TPU v7x, 256 devices: a whole 4x4x8 slice. The times are simulated.
256 devices in a mesh: copy: 32 (over z, y_hi, core), table: 8 (over y_lo, x).
Axes of the slice: x: 4, y: 4 (y_hi: 2, y_lo: 2; y = y_hi * 2 + y_lo), z: 8, core: 2. Of those that a mesh axis runs over, the one named last changes fastest.
Arguments:
- pooled: bfloat16 [8192, 40, 128], P('copy', 'table'), may hold values from -6 to 6
- slot_of_table: int32 [26], replicated, may hold values from 0 to 39, as said below
- partner: int32 [32], replicated, may hold values from 0 to 31, as said below
- labels: int32 [8192], P('copy'), may hold values 0 or 1
- w_first: bfloat16 [32, 3328, 4096], P('copy', None, 'table'), may hold values from -0.109375 to 0.109375
- b_first: bfloat16 [32, 4096], P('copy', 'table'), may hold values from -3 to 3
- w_head: bfloat16 [32, 4096], P('copy', 'table'), may hold values from -0.1875 to 0.1875
Outputs:
- pooled_grad: bfloat16 [40, 128, 8192], P('table', None, 'copy')
- grad_first: bfloat16 [32, 3328, 4096], P('copy', None, 'table')
- grad_bias: float32 [32, 4096], P('copy', 'table')
- grad_head: float32 [32, 4096], P('copy', 'table')
- loss_mean: float32 [32], P('copy')
Inputs may be any that keep to these rules, and one draw needn't show every extreme that they name: The slots are distinct; table t lies on the device of index slot_of_table[t] // 5 of the table axis; slots 0 and 39 are always used. A pairing: partner[partner[c]] == c and partner[c] != c.
All inputs are finite; a program needn't handle non-finite values. No bound on the sum of `labels` on one device may be relied on, other than what follows from the above.
Results may differ from a plain program's by a relative error of at most 0.017.
Values may be sent and summed in bfloat16 or wider, within the bound.
A program may use at most 64 MiB of HBM per device.

v0:
```python
import jax
import jax.numpy as jnp
from jax import lax
from jax.sharding import PartitionSpec as P


def swish_parts(pre_value):
    sigmoid_v = jax.nn.sigmoid(pre_value)
    return (pre_value * sigmoid_v, sigmoid_v * (1.0 + pre_value * (1.0 - sigmoid_v)))


def relay_weights(packed, partner):
    copy_count = lax.axis_size("copy")
    first_hop = lax.all_to_all(
        packed.reshape(copy_count, -1), "copy", split_axis=0, concat_axis=0, tiled=True
    )
    second_hop = lax.all_to_all(
        jnp.take(first_hop, partner, axis=0), "copy", split_axis=0, concat_axis=0, tiled=True
    )
    return second_hop.reshape(-1)


def own_features(pooled, slot_of_table, row_count, feature_count):
    gathered = lax.all_gather(pooled, "table", axis=1, tiled=True)
    return jnp.take(gathered, slot_of_table, axis=1).reshape(row_count, feature_count)


def split_pack(peer_packed, feature_count, unit_width):
    weight_size = feature_count * unit_width
    peer_weights = peer_packed[:weight_size].reshape(feature_count, unit_width)
    peer_bias = peer_packed[weight_size : weight_size + unit_width]
    peer_head = peer_packed[weight_size + unit_width :]
    return (peer_weights, peer_bias, peer_head)


def on_device(pooled, slot_of_table, partner, labels, w_first, b_first, w_head):
    row_count = pooled.shape[0]
    local_slots = pooled.shape[1]
    emb_width = pooled.shape[2]
    weights = w_first[0]
    bias_local = b_first[0]
    head_local = w_head[0]
    feature_count = weights.shape[0]
    unit_width = weights.shape[1]
    targets = labels.astype(jnp.float32)
    packed = jnp.concatenate([weights.reshape(-1), bias_local, head_local])
    features = own_features(pooled, slot_of_table, row_count, feature_count)
    own_pre = jnp.dot(features, weights, preferred_element_type=jnp.float32)
    peer_weights, other_bias, other_head = split_pack(
        relay_weights(packed, partner), feature_count, unit_width
    )
    other_pre = jnp.dot(features, peer_weights, preferred_element_type=jnp.float32)
    head_wide = head_local.astype(jnp.float32)
    activation, derivative = swish_parts(own_pre + bias_local.astype(jnp.float32)[None, :])
    other_act, other_slope = swish_parts(other_pre + other_bias.astype(jnp.float32)[None, :])
    own_partial = jnp.sum(activation * head_wide[None, :], axis=1)
    other_partial = jnp.sum(other_act * other_head.astype(jnp.float32)[None, :], axis=1)
    student_logit, other_logit = lax.psum((own_partial, other_partial), "table")
    soft_target = jax.nn.sigmoid(other_logit)
    loss_mean = jnp.mean(
        2.0 * jax.nn.softplus(student_logit) - targets * student_logit - soft_target * student_logit
    )
    logit_grad = 2.0 * jax.nn.sigmoid(student_logit) - targets - soft_target
    grad_pre = logit_grad[:, None] * head_wide[None, :] * derivative
    grad_low = grad_pre.astype(jnp.bfloat16)
    grad_first = lax.dot_general(
        features, grad_low, (((0,), (0,)), ((), ())), preferred_element_type=jnp.float32
    ).astype(jnp.bfloat16)
    grad_bias = jnp.sum(grad_pre, axis=0)
    grad_head = jnp.sum(logit_grad[:, None] * activation, axis=0)
    feature_grad = lax.dot_general(
        grad_low, weights, (((1,), (1,)), ((), ())), preferred_element_type=jnp.float32
    )
    table_count = slot_of_table.shape[0]
    by_table = feature_grad.reshape(row_count, table_count, emb_width)
    slot_total = local_slots * lax.axis_size("table")
    selector = (jnp.arange(slot_total, dtype=jnp.int32)[:, None] == slot_of_table[None, :]).astype(
        jnp.float32
    )
    placed = jnp.einsum("st,gte->seg", selector, by_table, precision=lax.Precision.HIGHEST)
    summed = lax.psum_scatter(
        placed.reshape(lax.axis_size("table") * (local_slots * emb_width), row_count).astype(
            jnp.bfloat16
        ),
        "table",
        scatter_dimension=0,
        tiled=True,
    )
    pooled_grad = summed.reshape(local_slots, emb_width, row_count)
    return (pooled_grad, grad_first[None], grad_bias[None], grad_head[None], loss_mean.reshape(1))


def solution(mesh):
    in_specs = (
        P("copy", "table", None),
        P(),
        P(),
        P("copy"),
        P("copy", None, "table"),
        P("copy", "table"),
        P("copy", "table"),
    )
    out_specs = (
        P("table", None, "copy"),
        P("copy", None, "table"),
        P("copy", "table"),
        P("copy", "table"),
        P("copy"),
    )
    return jax.shard_map(
        on_device, mesh=mesh, in_specs=in_specs, out_specs=out_specs, check_vma=False
    )
```

profile of v0, /device:TPU:1, one launch (start us, length us, event | category | flops | bytes accessed | tf_op | source)
XLA Modules:
  0.0 402.1 jit_solution(8117370246467826845)
XLA Ops:
  8.6 3.7 copy.33
  12.3 3.9 pad_maximum_fusion
  16.2 6.0 %all_to_all.16 = bf16[32,1,53280]{2,1,0:T(2,128)(2,1)} reshape(bf16[1704960]{0:T(1024)(128)(2,1)S(1)} %pad_maximum_fusion) | data formatting | bytes 6819840 | tf_op jit(solution)/shard_map/all_to_all | solution.py:14
  22.7 21.2 %reduce.4 = bf16[32,53280]{1,0:T(8,128)(2,1)S(1)} reduce(bf16[32,1,53280]{2,1,0:T(2,128)(2,1)} %all_to_all.16, bf16[]{:T(256)} %broadcast.118), dimensions={1}, to_apply=%all_to_all.16.reduce_sub_computation | reduce | bytes 6819842 | tf_op jit(solution)/shard_map/all_to_all | solution.py:14
  43.9 3.6 reshape.136
  47.5 12.9 %all-to-all-start = ((bf16[32,2,26640]{2,1,0:T(2,128)(2,1)}), bf16[32,2,26640]{2,1,0:T(2,128)(2,1)S(1)}, u32[]{:S(2)}, u32[]{:S(2)}) async-start(bf16[32,2,26640]{2,1,0:T(2,128)(2,1)} %reshape.136), calls=%async_computation | async-start | bytes 6848512 | tf_op jit(solution)/shard_map/all_to_all | solution.py:14
  60.5 80.0 %all-to-all-done = bf16[32,2,26640]{2,1,0:T(2,128)(2,1)S(1)} async-done(((bf16[32,2,26640]{2,1,0:T(2,128)(2,1)}), bf16[32,2,26640]{2,1,0:T(2,128)(2,1)S(1)}, u32[]{:S(2)}, u32[]{:S(2)}) %all-to-all-start) | async-done | bytes 3409952 | tf_op jit(solution)/shard_map/all_to_all | solution.py:14
  140.5 17.1 %reshape.137 = bf16[32,1,53280]{2,1,0:T(2,128)(2,1)} reshape(bf16[32,2,26640]{2,1,0:T(2,128)(2,1)S(1)} %all-to-all-done) | data formatting | bytes 6819840
  160.9 4.6 %gather_fusion.1 = bf16[32,53280]{1,0:T(8,128)(2,1)} fusion(bf16[32,53280]{1,0:T(8,128)(2,1)S(1)} %bitcast.42, s32[1024]{0:T(1024)S(1)} %pad_clamp_fusion), kind=kCustom, calls=%fused_computation.1 | custom fusion | bytes 6819968 | tf_op jit(solution)/shard_map/jit(_take)/gather | solution.py:18
  167.9 4.0 reduce.5
  171.9 5.3 %reshape.138 = bf16[32,2,26640]{2,1,0:T(2,128)(2,1)} reshape(bf16[32,53280]{1,0:T(8,128)(2,1)} %reduce.5) | data formatting | bytes 6819840
  177.2 5.0 %all-to-all-start.1 = ((bf16[32,2,26640]{2,1,0:T(2,128)(2,1)}), bf16[32,2,26640]{2,1,0:T(2,128)(2,1)}, u32[]{:S(2)}, u32[]{:S(2)}) async-start(bf16[32,2,26640]{2,1,0:T(2,128)(2,1)} %reshape.138), calls=%async_computation.1 | async-start | bytes 6848512 | tf_op jit(solution)/shard_map/all_to_all | solution.py:17
  183.2 56.0 %all-gather.2.cloned.1.call-done = bf16[256,40,128]{2,0,1:T(8,128)(2,1)} async-done(((bf16[256,5,128]{2,0,1:T(8,128)(2,1)}), bf16[256,40,128]{2,0,1:T(8,128)(2,1)}) %all-gather.2.cloned.1.call-update) | async-done | bytes 2621456 | tf_op jit(solution)/shard_map/all_gather | solution.py:24
  245.9 3.9 copy.23
  255.9 7.0 %all-to-all-done.1 = bf16[32,2,26640]{2,1,0:T(2,128)(2,1)} async-done(((bf16[32,2,26640]{2,1,0:T(2,128)(2,1)}), bf16[32,2,26640]{2,1,0:T(2,128)(2,1)}, u32[]{:S(2)}, u32[]{:S(2)}) %all-to-all-start.1) | async-done | bytes 3409952 | tf_op jit(solution)/shard_map/all_to_all | solution.py:17
  262.9 22.9 %reshape.139 = bf16[32,1,53280]{2,1,0:T(2,128)(2,1)} reshape(bf16[32,2,26640]{2,1,0:T(2,128)(2,1)} %all-to-all-done.1) | data formatting | bytes 6819840
  285.9 20.6 %reduce.2 = bf16[32,53280]{1,0:T(8,128)(2,1)S(1)} reduce(bf16[32,1,53280]{2,1,0:T(2,128)(2,1)} %reshape.139, bf16[]{:T(256)} %constant.46), dimensions={1}, to_apply=%all_to_all.15.reduce_sub_computation | reduce | bytes 6819842 | tf_op jit(solution)/shard_map/all_to_all | solution.py:17
  306.4 5.3 %reshape.134 = bf16[1704960]{0:T(1024)(128)(2,1)} reshape(bf16[32,53280]{1,0:T(8,128)(2,1)S(1)} %reduce.2) | data formatting | bytes 6819840
  312.5 6.6 %slice.12 = bf16[3330,512]{1,0:T(8,128)(2,1)} reshape(bf16[1704960]{0:T(1024)(128)(2,1)} %reshape.134) | data formatting | bytes 6819840 | tf_op jit(solution)/shard_map/slice | solution.py:30
  319.1 3.9 multiply_reduce_fusion.1
  323.0 14.7 %all-reduce = (f32[256]{0:T(256)S(1)}, f32[256]{0:T(256)S(1)}) all-reduce(f32[256]{0:T(256)S(1)} %get-tuple-element.18, f32[256]{0:T(256)S(1)} %multiply_reduce_fusion.1), channel_id=1, replica_groups=mesh['copy'=32,'table'=8] {'table'}, use_global_device_ids=true, to_apply=%region_1.2 | all-reduce | flops 512 | bytes 4096 | tf_op jit(solution)/shard_map/psum | solution.py:58
  340.6 5.3 %convert_bitcast_fusion = bf16[40,128,256]{1,0,2:T(8,128)(2,1)S(1)} fusion(f32[256,26,128]{2,0,1:T(8,128)S(1)} %fusion.18, s32[26]{0:T(128)S(1)} %copy-done.5), kind=kOutput, calls=%fused_computation.13 | convolution fusion | flops 410256384 | bytes 6029416 | tf_op jit(solution)/shard_map/st,gte->seg/dot_general | solution.py:80
  350.9 4.4 %fusion = bf16[1,3328,512]{2,1,0:T(8,128)(2,1)} fusion(bf16[256,3328]{0,1:T(8,128)(2,1)} %bitcast_select_fusion.1, f32[256,512]{1,0:T(8,128)S(1)} %copy-done.3, f32[256]{0:T(256)S(1)} %get-tuple-element.17, f32[512]{0:T(512)S(1)} %mul.67), kind=kOutput, calls=%fused_computation.3 | convolution fusion | flops 875429888 | bytes 5639168 | tf_op jit(solution)/shard_map/dot_general | solution.py:66
  355.3 38.8 %reduce-scatter.4.cloned.1.call-done = bf16[640,256]{1,0:T(8,128)(2,1)} async-done(((bf16[5120,256]{1,0:T(8,128)(2,1)}), bf16[640,256]{1,0:T(8,128)(2,1)}) %reduce-scatter.4.cloned.1.call-update) | async-done | bytes 327696 | tf_op jit(solution)/shard_map/reduce_scatter | solution.py:81
  (42 shorter events, 29.3 us)
Async XLA Ops:
  47.5 12.9 %copy-start.6 = (s32[32]{0:T(128)S(1)}, s32[32]{0:T(128)}, u32[]{:S(2)}) copy-start(s32[32]{0:T(128)} %param.9) | copy-start | bytes 388
  47.5 92.9 %all-to-all-start = ((bf16[32,2,26640]{2,1,0:T(2,128)(2,1)}), bf16[32,2,26640]{2,1,0:T(2,128)(2,1)S(1)}, u32[]{:S(2)}, u32[]{:S(2)}) async-start(bf16[32,2,26640]{2,1,0:T(2,128)(2,1)} %reshape.136), calls=%async_computation | async-start | bytes 6848512 | tf_op jit(solution)/shard_map/all_to_all | solution.py:14
  177.2 5.9 %copy-start.5 = (s32[26]{0:T(128)S(1)}, s32[26]{0:T(128)}, u32[]{:S(2)}) copy-start(s32[26]{0:T(128)} %param.8) | copy-start | bytes 316
  177.2 85.7 %all-to-all-start.1 = ((bf16[32,2,26640]{2,1,0:T(2,128)(2,1)}), bf16[32,2,26640]{2,1,0:T(2,128)(2,1)}, u32[]{:S(2)}, u32[]{:S(2)}) async-start(bf16[32,2,26640]{2,1,0:T(2,128)(2,1)} %reshape.138), calls=%async_computation.1 | async-start | bytes 6848512 | tf_op jit(solution)/shard_map/all_to_all | solution.py:17
  182.2 56.9 %all-gather.2.cloned.1.call-start = ((), (), s32[]{:S(2)}) async-start(), calls=%async_computation.3 | async-start | bytes 2949120 | tf_op jit(solution)/shard_map/all_gather | solution.py:24
  183.0 211.1 %reduce-scatter.4.cloned.1.call-start = ((), (), s32[]{:S(2)}) async-start(), calls=%async_computation.4 | async-start | bytes 2949120 | tf_op jit(solution)/shard_map/reduce_scatter | solution.py:81
  245.9 3.9 copy-start
  249.8 3.5 copy-start.2
  319.1 18.6 %copy-start.4 = (s32[256]{0:T(256)S(1)}, s32[256]{0:T(256)}, u32[]{:S(2)}) copy-start(s32[256]{0:T(256)} %param.10) | copy-start | bytes 3076
  319.1 19.2 %copy-start.1 = (bf16[1,3328,512]{2,1,0:T(8,128)(2,1)S(1)}, bf16[1,3328,512]{2,1,0:T(8,128)(2,1)}, u32[]{:S(2)}) copy-start(bf16[1,3328,512]{2,1,0:T(8,128)(2,1)} %param.11) | copy-start | bytes 10223620
  345.8 4.1 %copy-start.3 = (f32[256,512]{1,0:T(8,128)S(1)}, f32[256,512]{1,0:T(8,128)}, u32[]{:S(2)}) copy-start(f32[256,512]{1,0:T(8,128)} %get-tuple-element.19) | copy-start | bytes 1572868
Sparse Core Ops, SparseCore 0:
  184.9 54.2 all-gather.1
  349.5 44.5 reduce-scatter.3
where the time goes:
time: 407 us; the launch traced here: 402 us
  waiting for transfers between devices  182 us (45%)
  local copies, waits for them, and re-layouts  91.8 us (23%)
  other arithmetic  59.8 us (15%)
  matrix products  19.3 us (5%)
  starting transfers between devices  18 us (4%)
  between operations  16 us (4%)
  blocking collectives  14.7 us (4%)
    all_to_all x1, waiting for transfers between devices, relay_weights(): lax.all_to_all(packed.reshape(copy_count, -1), 'copy', split_axis=0, conc...  80 us
    unnamed x22, local copies, waits for them, and re-layouts  64.8 us
    all_gather x1, waiting for transfers between devices, own_features(): gathered = lax.all_gather(pooled, 'table', axis=1, tiled=True)  56 us
    reduce_scatter x1, waiting for transfers between devices, on_device(): lax.psum_scatter(placed.reshape(lax.axis_size('table') * (local_slots * e...  38.8 us
    all_to_all x1, other arithmetic, relay_weights(): lax.all_to_all(packed.reshape(copy_count, -1), 'copy', split_axis=0, conc...  21.2 us
    all_to_all x1, other arithmetic, relay_weights(): lax.all_to_all(jnp.take(first_hop, partner, axis=0), 'copy', split_axis=0...  20.6 us
    psum x1, blocking collectives, on_device(): student_logit, other_logit = lax.psum((own_partial, other_partial), 'table')  14.7 us
    all_to_all x1, starting transfers between devices, relay_weights(): lax.all_to_all(packed.reshape(copy_count, -1), 'copy', split_axis=0, conc...  12.9 us
  transfers between devices with their start and end apart: 4, of which 4 were waited for; matrix products, arithmetic and copies ran while one was open for 6% of the time, Pallas kernels for 0%

commit v1 on v0

v1 whole, which is shorter than its diff:
```python
import jax
import jax.numpy as jnp
from jax import lax
from jax.experimental import pallas as pl
from jax.experimental.pallas import tpu as pltpu
from jax.sharding import PartitionSpec as P

MESH = pl.DeviceIdType.MESH
F32, BF16 = jnp.float32, jnp.bfloat16
NT, NC = 8, 32
TAB, EMB, SLOTS, LOCAL = 26, 128, 40, 5
ROWS, HID, FEAT = 256, 512, 3328
RB = ROWS // NT
EB = EMB // NT
CH = 256
NCHUNK = FEAT // CH


def relay_copy(t):
    return jnp.where(t < 24, (t // 3) * 4 + t % 3, jnp.where(t == 24, 3, 19))


def kernel(
    slot_s, partner_s, inv_s, labels_v, pooled, w_hbm, b_v, h_v,
    pg_out, gf_out, gb_out, gh_out, loss_out,
    w_v, feat, feat_t, by_slot, relay_in, relay_out, act_v, a32_v, low_v, gt_v, part_in, sums, placed,
    gf_v, lg_own, lg_in, tl_own, tl_in,
    w_sem, gf_sem,
    a_send, a_recv, ag_send, ag_recv, c_send, c_recv, d_send, d_recv, tg_send, tg_recv,
    l_send, l_recv, t_send, t_recv, r_send, r_recv, z_send, z_recv,
):
    c = lax.axis_index("copy")
    k = lax.axis_index("table")
    my_rows = pl.ds(pl.multiple_of(k * RB, RB), RB)
    zq = lax.rem(c, 4)
    my_t = jnp.where(zq < 3, (c // 4) * 3 + zq, jnp.where(c == 3, 24, 25))
    is_relay = jnp.logical_or(zq < 3, jnp.logical_or(c == 3, c == 19))

    w_copy = pltpu.make_async_copy(w_hbm, w_v, w_sem)
    w_copy.start()

    barrier = pltpu.get_barrier_semaphore()

    def greet_table(d, _):
        pl.semaphore_signal(barrier, inc=1, device_id=(c, lax.rem(k + d, NT)), device_id_type=MESH)
        return 0

    def greet_copy(d, _):
        pl.semaphore_signal(barrier, inc=1, device_id=(lax.rem(c + d, NC), k), device_id_type=MESH)
        return 0

    lax.fori_loop(1, NT, greet_table, 0)
    lax.fori_loop(1, NC, greet_copy, 0)
    pl.semaphore_wait(barrier, NT - 1 + NC - 1)

    def remote(src, dst, send, recv, copy, table):
        return pltpu.make_async_remote_copy(
            src_ref=src, dst_ref=dst, send_sem=send, recv_sem=recv, device_id=(copy, table), device_id_type=MESH
        )

    def over_table(fn):
        def body(d, _):
            fn(d, lax.rem(k + d, NT))
            return 0

        lax.fori_loop(1, NT, body, 0)

    def take(ref, sem):
        pltpu.make_async_copy(ref, ref, sem).wait()

    def a_copy(d, j):
        rows = pl.ds(pl.multiple_of(j * RB, RB), RB)
        return remote(pooled.at[:, rows, :], by_slot.at[pl.ds(k * LOCAL, LOCAL)], a_send.at[d], a_recv, c, j)

    over_table(lambda d, j: a_copy(d, j).start())
    pltpu.make_async_copy(pooled.at[:, my_rows, :], by_slot.at[pl.ds(k * LOCAL, LOCAL)], a_recv).start()
    take(by_slot, a_recv)
    for t in range(TAB):
        feat[my_rows, t * EMB : (t + 1) * EMB] = by_slot[slot_s[t]]

    def c_copy(i):
        t = lax.rem(i + my_t, TAB)
        target = relay_copy(t)
        src = feat.at[my_rows, pl.ds(pl.multiple_of(t * EMB, EMB), EMB)]
        return src, target, remote(src, relay_in.at[c], c_send.at[i], c_recv, target, k)

    def c_start(i, _):
        src, target, copy = c_copy(i)

        @pl.when(target != c)
        def _():
            copy.start()

        @pl.when(target == c)
        def _():
            pltpu.make_async_copy(src, relay_in.at[c], c_recv).start()

        return 0

    lax.fori_loop(0, TAB, c_start, 0)

    def ag_copy(buf, send, recv, d, j):
        return remote(buf.at[my_rows], buf.at[my_rows], send.at[d], recv.at[k], c, j)

    over_table(lambda d, j: ag_copy(feat, ag_send, ag_recv, d, j).start())

    def d_copy(d, p):
        t = pl.ds(pl.multiple_of(my_t * EMB, EMB), EMB)
        return remote(relay_out.at[p], feat_t.at[my_rows, t], d_send.at[d], d_recv, p, k)

    @pl.when(is_relay)
    def _():
        take(relay_in, c_recv)

        def pick(p, _):
            relay_out[p] = relay_in[partner_s[p]]
            return 0

        lax.fori_loop(0, NC, pick, 0, unroll=4)

        def d_start(d, _):
            d_copy(d, lax.rem(c + d, NC)).start()
            return 0

        lax.fori_loop(1, NC, d_start, 0)
        t = pl.ds(pl.multiple_of(my_t * EMB, EMB), EMB)
        pltpu.make_async_copy(relay_out.at[c], feat_t.at[my_rows, t], d_recv).start()

    take(feat_t.at[my_rows], d_recv)
    over_table(lambda d, j: ag_copy(feat_t, tg_send, tg_recv, d, j).start())

    def ag_wait(buf, send, recv):
        def body(d, j):
            rows = pl.ds(pl.multiple_of(j * RB, RB), RB)
            take(buf.at[rows], recv.at[j])

        over_table(body)

    def head_row(total):
        return jnp.sum(jnp.transpose(total), axis=0, keepdims=True)

    ag_wait(feat, ag_send, ag_recv)
    w_copy.wait()
    total = jnp.zeros((ROWS, EMB), F32)
    for n in range(HID // CH):
        cols = slice(n * CH, (n + 1) * CH)
        head = h_v[:, cols].astype(F32)
        pre = jnp.dot(feat[...], w_v[:, cols], preferred_element_type=F32) + b_v[:, cols].astype(F32)
        sig = jax.nn.sigmoid(pre)
        act = pre * sig
        act_v[:, cols] = act
        a32 = head * (sig * (1.0 + pre * (1.0 - sig)))
        a32_v[:, cols] = a32
        low_v[:, cols] = a32.astype(BF16)
        weighed = act * head
        total = total + (weighed[:, :EMB] + weighed[:, EMB:])
    lg_own[...] = jnp.zeros_like(lg_own)
    lg_own[0:1, :] = head_row(total)

    def gt_step(i, _):
        rows = pl.ds(pl.multiple_of(i * CH, CH), CH)
        g = lax.dot_general(w_v[rows, :], low_v[...], (((1,), (1,)), ((), ())), preferred_element_type=F32)
        gt_v[pl.ds(i * 2, 2)] = g.astype(BF16).reshape(2, EMB, ROWS)
        return 0

    lax.fori_loop(0, NCHUNK, gt_step, 0)

    def r_copy(d, j):
        part = pl.ds(pl.multiple_of(j * EB, EB), EB)
        return remote(gt_v.at[:, part, :], part_in.at[k], r_send.at[d], r_recv, c, j)

    over_table(lambda d, j: r_copy(d, j).start())
    my_part = pl.ds(pl.multiple_of(k * EB, EB), EB)
    pltpu.make_async_copy(gt_v.at[:, my_part, :], part_in.at[k], r_recv).start()

    ag_wait(feat_t, tg_send, tg_recv)
    total = jnp.zeros((ROWS, EMB), F32)
    for n in range(HID // CH):
        cols = slice(n * CH, (n + 1) * CH)
        pre = jnp.dot(feat_t[...], w_v[:, cols], preferred_element_type=F32) + b_v[:, cols].astype(F32)
        weighed = pre * jax.nn.sigmoid(pre) * h_v[:, cols].astype(F32)
        total = total + (weighed[:, :EMB] + weighed[:, EMB:])
    lg_own[1:2, :] = head_row(total)

    lg_in[k] = lg_own[...]

    def l_copy(d, j):
        return remote(lg_own, lg_in.at[k], l_send.at[d], l_recv, c, j)

    over_table(lambda d, j: l_copy(d, j).start())
    take(lg_in.at[pl.ds(0, NT - 1)], l_recv)
    tl_own[...] = jnp.sum(lg_in[...], axis=0)
    tl_in[c] = tl_own[...]

    def t_copy(d):
        return remote(tl_own, tl_in.at[c], t_send.at[d], t_recv, lax.rem(c + d, NC), k)

    def t_start(d, _):
        t_copy(d).start()
        return 0

    lax.fori_loop(1, NC, t_start, 0)
    take(tl_in.at[pl.ds(0, NC - 1)], t_recv)

    z = tl_own[0:1, :]
    q = jax.nn.sigmoid(tl_in[partner_s[c]][1:2, :])
    y = labels_v[...].astype(F32)
    soft = jnp.maximum(z, 0.0) + jnp.log1p(jnp.exp(-jnp.abs(z)))
    loss_out[0] = jnp.sum(2.0 * soft - y * z - q * z) * (1.0 / ROWS)
    lg = 2.0 * jax.nn.sigmoid(z) - y - q
    lg_col = jnp.transpose(jnp.broadcast_to(lg, (EMB, ROWS)))
    for n in range(HID // EMB):
        cols = slice(n * EMB, (n + 1) * EMB)
        grad_pre = lg_col * a32_v[:, cols]
        low_v[:, cols] = grad_pre.astype(BF16)
        gb_out[:, cols] = jnp.sum(grad_pre, axis=0, keepdims=True)
        gh_out[:, cols] = jnp.sum(lg_col * act_v[:, cols], axis=0, keepdims=True)

    def gf_copy(i):
        rows = pl.ds(pl.multiple_of(i * CH, CH), CH)
        return pltpu.make_async_copy(gf_v.at[rows], gf_out.at[rows], gf_sem.at[i])

    def gf_step(i, _):
        rows = pl.ds(pl.multiple_of(i * CH, CH), CH)
        g = lax.dot_general(feat[:, rows], low_v[...], (((0,), (0,)), ((), ())), preferred_element_type=F32)
        gf_v[rows, :] = g.astype(BF16)
        gf_copy(i).start()
        return 0

    lax.fori_loop(0, NCHUNK, gf_step, 0)

    take(part_in, r_recv)
    sums[TAB] = jnp.zeros((EB, ROWS), BF16)

    def sum_step(t, _):
        total = part_in[0, t].astype(F32)
        for j in range(1, NT):
            total = total + part_in[j, t].astype(F32)
        sums[t] = (total * lg).astype(BF16)
        return 0

    lax.fori_loop(0, TAB, sum_step, 0, unroll=2)

    def place(s, _):
        placed[s] = sums[inv_s[s]]
        return 0

    lax.fori_loop(0, SLOTS, place, 0, unroll=4)

    def z_copy(d, j):
        return remote(placed.at[pl.ds(j * LOCAL, LOCAL)], pg_out.at[:, my_part, :], z_send.at[d], z_recv, c, j)

    over_table(lambda d, j: z_copy(d, j).start())
    pltpu.make_async_copy(placed.at[pl.ds(k * LOCAL, LOCAL)], pg_out.at[:, my_part, :], z_recv).start()
    take(pg_out, z_recv)

    over_table(lambda d, j: a_copy(d, j).wait_send())

    def c_wait(i, _):
        _, target, copy = c_copy(i)

        @pl.when(target != c)
        def _():
            copy.wait_send()

        return 0

    lax.fori_loop(0, TAB, c_wait, 0)
    over_table(lambda d, j: ag_copy(feat, ag_send, ag_recv, d, j).wait_send())

    @pl.when(is_relay)
    def _():
        def d_wait(d, _):
            d_copy(d, lax.rem(c + d, NC)).wait_send()
            return 0

        lax.fori_loop(1, NC, d_wait, 0)

    over_table(lambda d, j: ag_copy(feat_t, tg_send, tg_recv, d, j).wait_send())
    over_table(lambda d, j: l_copy(d, j).wait_send())

    def t_wait(d, _):
        t_copy(d).wait_send()
        return 0

    lax.fori_loop(1, NC, t_wait, 0)
    over_table(lambda d, j: r_copy(d, j).wait_send())
    over_table(lambda d, j: z_copy(d, j).wait_send())

    def gf_wait(i, _):
        gf_copy(i).wait()
        return 0

    lax.fori_loop(0, NCHUNK, gf_wait, 0)


def on_device(pooled, slot_of_table, partner, labels, w_first, b_first, w_head):
    slots = jnp.arange(SLOTS, dtype=jnp.int32)[:, None]
    inverse = jnp.min(
        jnp.where(slots == slot_of_table[None, :], jnp.arange(TAB, dtype=jnp.int32)[None, :], TAB), axis=1
    )
    vmem = pl.BlockSpec(memory_space=pltpu.VMEM)
    smem = pl.BlockSpec(memory_space=pltpu.SMEM)
    hbm = pl.BlockSpec(memory_space=pl.ANY)
    dma = pltpu.SemaphoreType.DMA
    pg, gf, gb, gh, loss = pl.pallas_call(
        kernel,
        out_shape=(
            jax.ShapeDtypeStruct((LOCAL, EMB, ROWS), BF16),
            jax.ShapeDtypeStruct((FEAT, HID), BF16),
            jax.ShapeDtypeStruct((1, HID), F32),
            jax.ShapeDtypeStruct((1, HID), F32),
            jax.ShapeDtypeStruct((1,), F32),
        ),
        in_specs=[smem, smem, smem, vmem, hbm, hbm, vmem, vmem],
        out_specs=(vmem, hbm, vmem, vmem, smem),
        scratch_shapes=[
            pltpu.VMEM((FEAT, HID), BF16),
            pltpu.VMEM((ROWS, FEAT), BF16),
            pltpu.VMEM((ROWS, FEAT), BF16),
            pltpu.VMEM((SLOTS, RB, EMB), BF16),
            pltpu.VMEM((NC, RB, EMB), BF16),
            pltpu.VMEM((NC, RB, EMB), BF16),
            pltpu.VMEM((ROWS, HID), F32),
            pltpu.VMEM((ROWS, HID), F32),
            pltpu.VMEM((ROWS, HID), BF16),
            pltpu.VMEM((TAB, EMB, ROWS), BF16),
            pltpu.VMEM((NT, TAB, EB, ROWS), BF16),
            pltpu.VMEM((TAB + 1, EB, ROWS), BF16),
            pltpu.VMEM((SLOTS, EB, ROWS), BF16),
            pltpu.VMEM((FEAT, HID), BF16),
            pltpu.VMEM((8, ROWS), F32),
            pltpu.VMEM((NT, 8, ROWS), F32),
            pltpu.VMEM((8, ROWS), F32),
            pltpu.VMEM((NC, 8, ROWS), F32),
            dma, dma((NCHUNK,)),
            dma((NT,)), dma,
            dma((NT,)), dma((NT,)),
            dma((TAB,)), dma,
            dma((NC,)), dma,
            dma((NT,)), dma((NT,)),
            dma((NT,)), dma,
            dma((NC,)), dma,
            dma((NT,)), dma,
            dma((NT,)), dma,
        ],
        compiler_params=pltpu.CompilerParams(
            collective_id=0, has_side_effects=True, vmem_limit_bytes=48 * 1024 * 1024
        ),
    )(
        slot_of_table, partner, inverse, labels.reshape(1, ROWS), jnp.transpose(pooled, (1, 0, 2)),
        w_first.reshape(FEAT, HID), b_first, w_head,
    )
    return pg, gf[None], gb, gh, loss


def solution(mesh):
    in_specs = (
        P("copy", "table", None), P(), P(), P("copy"), P("copy", None, "table"), P("copy", "table"), P("copy", "table"),
    )
    out_specs = (
        P("table", None, "copy"), P("copy", None, "table"), P("copy", "table"), P("copy", "table"), P("copy"),
    )
    return jax.shard_map(on_device, mesh=mesh, in_specs=in_specs, out_specs=out_specs, check_vma=False)
```

time: 407 us -> 129 us (0.32); the launches traced: 402 us -> 129 us
  waiting for transfers between devices: 182 us -> 0 us
  Pallas kernels: 0 us -> 118 us
  local copies, waits for them, and re-layouts: 91.8 us -> 7.95 us
  other arithmetic: 59.8 us -> 0.75 us
  matrix products: 19.3 us -> 0 us
  starting transfers between devices: 18 us -> 0 us
  blocking collectives: 14.7 us -> 0 us
  between operations: 16 us -> 2.4 us
    pallas_call x0 -> x1, Pallas kernels: none -> 118 us  [on_device(): pl.pallas_call(kernel, out_shape=(jax.ShapeDtypeStruct((LOCAL, EMB, ROWS)...]
    all_to_all x2 -> x0, waiting for transfers between devices: 87 us -> none  [the longest x1 80 us: relay_weights(): lax.all_to_all(packed.reshape(copy_count, -1), 'copy', split_axis=0, conc...]
    unnamed x22 -> x16, local copies, waits for them, and re-layouts: 64.8 us -> 7.95 us
    all_gather x1 -> x0, waiting for transfers between devices: 56 us -> none  [own_features(): gathered = lax.all_gather(pooled, 'table', axis=1, tiled=True)]
    all_to_all x2 -> x0, other arithmetic: 41.8 us -> none  [the longest x1 21.2 us: relay_weights(): lax.all_to_all(packed.reshape(copy_count, -1), 'copy', split_axis=0, conc...]
    reduce_scatter x1 -> x0, waiting for transfers between devices: 38.8 us -> none  [on_device(): lax.psum_scatter(placed.reshape(lax.axis_size('table') * (local_slots * e...]
    dot_general x5 -> x0, matrix products: 19.3 us -> none  [the longest x1 5.26 us: on_device(): jnp.einsum('st,gte->seg', selector, by_table, precision=lax.Precision.HIG...]
    all_to_all x2 -> x0, starting transfers between devices: 17.9 us -> none  [the longest x1 12.9 us: relay_weights(): lax.all_to_all(packed.reshape(copy_count, -1), 'copy', split_axis=0, conc...]
  transfers between devices with their start and end apart: 4 -> 0, of which waited for: 4 -> 0; matrix products, arithmetic and copies ran while one was open for 6% -> 0% of each run, Pallas kernels for 0% -> 0%
where the time goes in v1:
time: 129 us
  Pallas kernels  118 us (91%)
  local copies, waits for them, and re-layouts  7.95 us (6%)
  between operations  2.4 us (2%)
    pallas_call x1, Pallas kernels, on_device(): pl.pallas_call(kernel, out_shape=(jax.ShapeDtypeStruct((LOCAL, EMB, ROWS)...  118 us
    unnamed x16, local copies, waits for them, and re-layouts  7.95 us

profile of v1, /device:TPU:1, one launch (start us, length us, event | category | flops | bytes accessed | tf_op | source)
XLA Modules:
  0.0 128.8 jit_solution(15022432056202519844)
XLA Ops:
  0.6 0.7 select_reduce_fusion.inv_s
  1.4 0.0 copy-start
  1.4 1.0 copy-done
  2.3 0.0 copy-start.1
  2.4 0.7 copy-done.1
  3.0 0.0 copy-start.2
  3.0 0.7 copy-done.2
  3.7 0.0 copy-start.3
  3.7 0.7 copy-done.3
  4.4 0.0 copy-start.4
  4.4 0.7 copy-done.4
  5.0 0.0 copy-start.5
  5.1 0.7 copy-done.5
  5.7 117.7 %shard_map.110 = (bf16[5,128,256]{2,1,0:T(8,128)(2,1)S(1)}, bf16[3328,512]{1,0:T(8,128)(2,1)S(1)}, f32[1,512]{1,0:T(1,128)S(1)}, f32[1,512]{1,0:T(1,128)S(1)}, f32[1]{0:T(128)}) custom-call(s32[26]{0:T(128)S(1)} %copy-done.4, s32[32]{0:T(128)S(1)} %copy-done.5, s32[40]{0:T(128)S(1)} %select_reduce_fusion.inv_s, s32[1,256]{1,0:T(1,128)S(1)} %bitcast.6, ...), custom_call_target="tpu_custom_call" | custom-call | tf_op jit(solution)/shard_map/pallas_call | solution.py:306
  123.4 0.7 copy.17
  124.1 1.7 %copy.18 = bf16[1,3328,512]{2,1,0:T(8,128)(2,1)} copy(bf16[1,3328,512]{2,1,0:T(8,128)(2,1)S(1)} %bitcast.4) | data formatting | bytes 6815744
  125.9 0.6 copy.19
  126.4 0.6 copy.20
Async XLA Ops:
  1.4 1.0 copy-start
  2.3 0.7 copy-start.1
  3.0 0.7 copy-start.2
  3.7 0.7 copy-start.3
  4.4 0.7 copy-start.4
  5.0 0.7 copy-start.5

commit v2 on v1

v2 whole, which is shorter than its diff:
```python
import jax
import jax.numpy as jnp
from jax import lax
from jax.experimental import pallas as pl
from jax.experimental.pallas import tpu as pltpu
from jax.sharding import PartitionSpec as P

MESH = pl.DeviceIdType.MESH
F32, BF16 = jnp.float32, jnp.bfloat16
NT, NC = 8, 32
TAB, EMB, SLOTS, LOCAL = 26, 128, 40, 5
ROWS, HID, FEAT = 256, 512, 3328
RB = ROWS // NT
EB = EMB // NT
CH = 256
NCHUNK = FEAT // CH
HALF = FEAT // 2

A, B, BOTH = (0, RB // 2), (RB // 2, RB // 2), (0, RB)
ALL, LOW, HIGH = (0, FEAT), (0, HALF), (HALF, HALF)
TREE = (
    ((0, 0), (0, 1), A, ALL, "y"),
    ((0, 0), (0, 1), B, ALL, "y"),
    ((0, 0), (3, 0), BOTH, ALL, "right"),
    ((0, 0), (1, 0), BOTH, ALL, "left"),
    ((0, 1), (3, 1), A, ALL, "right"),
    ((0, 1), (1, 1), A, ALL, "left"),
    ((3, 0), (2, 0), BOTH, LOW, "right"),
    ((1, 0), (2, 0), BOTH, HIGH, "left"),
    ((3, 0), (3, 1), B, ALL, "y"),
    ((1, 0), (1, 1), B, ALL, "y"),
    ((3, 1), (2, 1), A, LOW, "right"),
    ((1, 1), (2, 1), A, HIGH, "left"),
    ((2, 0), (2, 1), B, ALL, "y"),
)
TREE_STEPS = (((), (0, 2, 3, 1)), ((0,), (4, 5)), ((2,), (6, 8)), ((3,), (7, 9)), ((4,), (10,)), ((5,), (11,)), ((6, 7), (12,)),
              ((1, 8, 9, 10, 11, 12), ()))


def relay_copy(t):
    return jnp.where(t < 24, (t // 3) * 4 + t % 3, jnp.where(t == 24, 3, 19))


def kernel(
    slot_h, partner_h, labels_h, pooled, w_hbm, b_h, h_h,
    feat, act_v, a32_v, lg_out, pg_out,
    w_v, feat_t, by_slot, relay_in, relay_out, low_v, gt_v, part_in, sums, placed,
    z_own, z_in, q_own, q_in, qs_own, qs_in, b_v, h_v, y_v, slot_s, partner_s, inv_v, inv_s,
    load_sem, inv_sem,
    a_send, a_recv, ag_send, ag_recv, c_send, c_recv, d_send, d_recv, tg_send, tg_recv,
    l_send, l_recv, m_send, m_recv, t_send, t_recv, r_send, r_recv, z_send, z_recv,
):
    c = lax.axis_index("copy")
    k = lax.axis_index("table")
    x, y = lax.rem(k, 4), k // 4
    my_rows = pl.ds(pl.multiple_of(k * RB, RB), RB)
    zq = lax.rem(c, 4)
    my_t = jnp.where(zq < 3, (c // 4) * 3 + zq, jnp.where(c == 3, 24, 25))
    is_relay = jnp.logical_or(zq < 3, jnp.logical_or(c == 3, c == 19))

    barrier = pltpu.get_barrier_semaphore()

    def greet_table(d, _):
        pl.semaphore_signal(barrier, inc=1, device_id=(c, lax.rem(k + d, NT)), device_id_type=MESH)
        return 0

    def greet_copy(d, _):
        pl.semaphore_signal(barrier, inc=1, device_id=(lax.rem(c + d, NC), k), device_id_type=MESH)
        return 0

    lax.fori_loop(1, NT, greet_table, 0)
    lax.fori_loop(1, NC, greet_copy, 0)

    loads = [
        pltpu.make_async_copy(src, dst, load_sem.at[i])
        for i, (src, dst) in enumerate(
            ((slot_h, slot_s), (partner_h, partner_s), (labels_h, y_v), (b_h, b_v), (h_h, h_v), (w_hbm, w_v))
        )
    ]
    for load in loads:
        load.start()
    pl.semaphore_wait(barrier, NT - 1 + NC - 1)

    def remote(src, dst, send, recv, copy, table):
        return pltpu.make_async_remote_copy(
            src_ref=src, dst_ref=dst, send_sem=send, recv_sem=recv, device_id=(copy, table), device_id_type=MESH
        )

    def over_table(fn):
        def body(d, _):
            fn(d, lax.rem(k + d, NT))
            return 0

        lax.fori_loop(1, NT, body, 0)

    def take(ref, sem):
        pltpu.make_async_copy(ref, ref, sem).wait()

    def share(step):
        return lax.rem(y + step[1], 2) * 4 + lax.rem(x + step[0], 4)

    target = {"y": share((0, 1)), "right": share((1, 0)), "left": share((3, 0))}

    def region(buf, origin, rows, cols):
        first = pl.multiple_of(share(origin) * RB + rows[0], RB // 2)
        return buf.at[pl.ds(first, rows[1]), pl.ds(cols[0], cols[1])]

    def tree_copy(buf, send, recv, i):
        origin, _, rows, cols, to = TREE[i]
        piece = region(buf, origin, rows, cols)
        return remote(piece, piece, send.at[i], recv.at[i], c, target[to])

    def tree_step(buf, send, recv, step):
        waits, starts = TREE_STEPS[step]
        for i in waits:
            _, origin, rows, cols, _ = TREE[i]
            take(region(buf, origin, rows, cols), recv.at[i])
        for i in starts:
            tree_copy(buf, send, recv, i).start()

    def a_copy(d, j):
        rows = pl.ds(pl.multiple_of(j * RB, RB), RB)
        return remote(pooled.at[:, rows, :], by_slot.at[pl.ds(k * LOCAL, LOCAL)], a_send.at[d], a_recv, c, j)

    over_table(lambda d, j: a_copy(d, j).start())
    pltpu.make_async_copy(pooled.at[:, my_rows, :], by_slot.at[pl.ds(k * LOCAL, LOCAL)], a_recv).start()
    for load in loads:
        load.wait()

    lane = lax.broadcasted_iota(jnp.int32, (8, EMB), 1)
    slots = jnp.full((8, EMB), SLOTS, jnp.int32)
    for t in range(TAB):
        slots = jnp.where(lane == t, slot_s[t], slots)
    for i in range(SLOTS // 8):
        found = jnp.where(lax.broadcasted_iota(jnp.int32, (8, EMB), 0) + 8 * i == slots, lane, TAB)
        inv_v[8 * i : 8 * i + 8, :] = jnp.broadcast_to(jnp.min(found, axis=1, keepdims=True), (8, EMB))
    inv_copy = pltpu.make_async_copy(inv_v, inv_s, inv_sem)
    inv_copy.start()

    take(by_slot, a_recv)
    for t in range(TAB):
        feat[my_rows, t * EMB : (t + 1) * EMB] = by_slot[slot_s[t]]

    tree_step(feat, ag_send, ag_recv, 0)

    def c_copy(i):
        t = lax.rem(i + my_t, TAB)
        to = relay_copy(t)
        src = feat.at[my_rows, pl.ds(pl.multiple_of(t * EMB, EMB), EMB)]
        return src, to, remote(src, relay_in.at[c], c_send.at[i], c_recv, to, k)

    def c_start(i, _):
        src, to, copy = c_copy(i)

        @pl.when(to != c)
        def _():
            copy.start()

        @pl.when(to == c)
        def _():
            pltpu.make_async_copy(src, relay_in.at[c], c_recv).start()

        return 0

    lax.fori_loop(0, TAB, c_start, 0)
    for step in range(1, 6):
        tree_step(feat, ag_send, ag_recv, step)

    my_cols = pl.ds(pl.multiple_of(my_t * EMB, EMB), EMB)

    def d_copy(d, p):
        return remote(relay_out.at[p], feat_t.at[my_rows, my_cols], d_send.at[d], d_recv, p, k)

    @pl.when(is_relay)
    def _():
        take(relay_in, c_recv)

        def pick(p, _):
            relay_out[p] = relay_in[partner_s[p]]
            return 0

        lax.fori_loop(0, NC, pick, 0, unroll=4)

        def d_start(d, _):
            d_copy(d, lax.rem(c + d, NC)).start()
            return 0

        lax.fori_loop(1, NC, d_start, 0)
        pltpu.make_async_copy(relay_out.at[c], feat_t.at[my_rows, my_cols], d_recv).start()

    for step in range(6, len(TREE_STEPS)):
        tree_step(feat, ag_send, ag_recv, step)

    def head_row(total):
        return jnp.sum(jnp.transpose(total), axis=0, keepdims=True)

    total = jnp.zeros((ROWS, EMB), F32)
    for n in range(HID // CH):
        cols = slice(n * CH, (n + 1) * CH)
        head = h_v[:, cols].astype(F32)
        pre = jnp.dot(feat[...], w_v[:, cols], preferred_element_type=F32) + b_v[:, cols].astype(F32)
        sig = jax.nn.sigmoid(pre)
        act = pre * sig
        act_v[:, cols] = act
        a32 = head * (sig * (1.0 + pre * (1.0 - sig)))
        a32_v[:, cols] = a32
        low_v[:, cols] = a32.astype(BF16)
        weighed = act * head
        total = total + (weighed[:, :EMB] + weighed[:, EMB:])
    z_own[...] = head_row(total)

    def gt_step(i, _):
        rows = pl.ds(pl.multiple_of(i * CH, CH), CH)
        g = lax.dot_general(w_v[rows, :], low_v[...], (((1,), (1,)), ((), ())), preferred_element_type=F32)
        gt_v[pl.ds(i * 2, 2)] = g.astype(BF16).reshape(2, EMB, ROWS)
        return 0

    lax.fori_loop(0, NCHUNK, gt_step, 0)

    z_in[k] = z_own[...]

    def l_copy(d, j):
        return remote(z_own, z_in.at[k], l_send.at[d], l_recv, c, j)

    over_table(lambda d, j: l_copy(d, j).start())

    def r_copy(d, j):
        part = pl.ds(pl.multiple_of(j * EB, EB), EB)
        return remote(gt_v.at[:, part, :], part_in.at[k], r_send.at[d], r_recv, c, j)

    over_table(lambda d, j: r_copy(d, j).start())
    my_part = pl.ds(pl.multiple_of(k * EB, EB), EB)
    pltpu.make_async_copy(gt_v.at[:, my_part, :], part_in.at[k], r_recv).start()

    take(feat_t.at[my_rows], d_recv)
    tree_step(feat_t, tg_send, tg_recv, 0)

    take(part_in, r_recv)
    inv_copy.wait()
    sums[TAB] = jnp.zeros((EB, ROWS), BF16)

    def sum_step(t, _):
        total = part_in[0, t].astype(F32)
        for j in range(1, NT):
            total = total + part_in[j, t].astype(F32)
        sums[t] = total.astype(BF16)
        return 0

    lax.fori_loop(0, TAB, sum_step, 0, unroll=2)

    def place(s, _):
        placed[s] = sums[inv_s[s, 0]]
        return 0

    lax.fori_loop(0, SLOTS, place, 0, unroll=4)

    def z_copy(d, j):
        return remote(placed.at[pl.ds(j * LOCAL, LOCAL)], pg_out.at[:, my_part, :], z_send.at[d], z_recv, c, j)

    over_table(lambda d, j: z_copy(d, j).start())
    pltpu.make_async_copy(placed.at[pl.ds(k * LOCAL, LOCAL)], pg_out.at[:, my_part, :], z_recv).start()

    for step in range(1, len(TREE_STEPS)):
        tree_step(feat_t, tg_send, tg_recv, step)
    total = jnp.zeros((ROWS, EMB), F32)
    for n in range(HID // CH):
        cols = slice(n * CH, (n + 1) * CH)
        pre = jnp.dot(feat_t[...], w_v[:, cols], preferred_element_type=F32) + b_v[:, cols].astype(F32)
        weighed = pre * jax.nn.sigmoid(pre) * h_v[:, cols].astype(F32)
        total = total + (weighed[:, :EMB] + weighed[:, EMB:])
    q_own[...] = head_row(total)
    q_in[k] = q_own[...]

    def m_copy(d, j):
        return remote(q_own, q_in.at[k], m_send.at[d], m_recv, c, j)

    over_table(lambda d, j: m_copy(d, j).start())
    take(z_in.at[pl.ds(0, NT - 1)], l_recv)
    take(q_in.at[pl.ds(0, NT - 1)], m_recv)
    qs_own[...] = jnp.sum(q_in[...], axis=0)
    qs_in[c] = qs_own[...]

    def t_copy(d):
        return remote(qs_own, qs_in.at[c], t_send.at[d], t_recv, lax.rem(c + d, NC), k)

    def t_start(d, _):
        t_copy(d).start()
        return 0

    lax.fori_loop(1, NC, t_start, 0)
    take(qs_in.at[pl.ds(0, NC - 1)], t_recv)

    z = jnp.sum(z_in[...], axis=0)
    q = jax.nn.sigmoid(qs_in[partner_s[c]])
    target_y = y_v[...].astype(F32)
    soft = jnp.maximum(z, 0.0) + jnp.log1p(jnp.exp(-jnp.abs(z)))
    lg_out[...] = jnp.zeros_like(lg_out)
    lg_out[0:1, :] = 2.0 * jax.nn.sigmoid(z) - target_y - q
    lg_out[1:2, :] = 2.0 * soft - target_y * z - q * z

    take(pg_out, z_recv)

    over_table(lambda d, j: a_copy(d, j).wait_send())

    def c_wait(i, _):
        _, to, copy = c_copy(i)

        @pl.when(to != c)
        def _():
            copy.wait_send()

        return 0

    lax.fori_loop(0, TAB, c_wait, 0)
    for i in range(len(TREE)):
        tree_copy(feat, ag_send, ag_recv, i).wait_send()
        tree_copy(feat_t, tg_send, tg_recv, i).wait_send()

    @pl.when(is_relay)
    def _():
        def d_wait(d, _):
            d_copy(d, lax.rem(c + d, NC)).wait_send()
            return 0

        lax.fori_loop(1, NC, d_wait, 0)

    def t_wait(d, _):
        t_copy(d).wait_send()
        return 0

    lax.fori_loop(1, NC, t_wait, 0)

    def rest(d, j):
        l_copy(d, j).wait_send()
        m_copy(d, j).wait_send()
        r_copy(d, j).wait_send()
        z_copy(d, j).wait_send()

    over_table(rest)


def finish(feat, act_v, a32_v, lg_v, pg_v, pg_out, gf_out, gb_out, gh_out, loss_out, low_v, gf_v, gf_sem):
    lg = lg_v[0:1, :]
    lg_col = jnp.transpose(jnp.broadcast_to(lg, (EMB, ROWS)))
    for n in range(HID // EMB):
        cols = slice(n * EMB, (n + 1) * EMB)
        grad_pre = lg_col * a32_v[:, cols]
        low_v[:, cols] = grad_pre.astype(BF16)
        gb_out[:, cols] = jnp.sum(grad_pre, axis=0, keepdims=True)
        gh_out[:, cols] = jnp.sum(lg_col * act_v[:, cols], axis=0, keepdims=True)

    def gf_copy(i):
        rows = pl.ds(pl.multiple_of(i * CH, CH), CH)
        return pltpu.make_async_copy(gf_v.at[rows], gf_out.at[rows], gf_sem.at[i])

    def gf_step(i, _):
        rows = pl.ds(pl.multiple_of(i * CH, CH), CH)
        g = lax.dot_general(feat[:, rows], low_v[...], (((0,), (0,)), ((), ())), preferred_element_type=F32)
        gf_v[rows, :] = g.astype(BF16)
        gf_copy(i).start()
        return 0

    lax.fori_loop(0, NCHUNK, gf_step, 0)
    loss_out[0] = jnp.sum(lg_v[1:2, :]) * (1.0 / ROWS)
    for s in range(LOCAL):
        pg_out[s] = (pg_v[s].astype(F32) * lg).astype(BF16)

    def gf_wait(i, _):
        gf_copy(i).wait()
        return 0

    lax.fori_loop(0, NCHUNK, gf_wait, 0)


def on_device(pooled, slot_of_table, partner, labels, w_first, b_first, w_head):
    vmem = pl.BlockSpec(memory_space=pltpu.VMEM)
    smem = pl.BlockSpec(memory_space=pltpu.SMEM)
    hbm = pl.BlockSpec(memory_space=pltpu.HBM)
    dma = pltpu.SemaphoreType.DMA
    tree = dma((len(TREE),))
    feat, act, a32, lg, sums = pl.pallas_call(
        kernel,
        out_shape=(
            jax.ShapeDtypeStruct((ROWS, FEAT), BF16),
            jax.ShapeDtypeStruct((ROWS, HID), F32),
            jax.ShapeDtypeStruct((ROWS, HID), F32),
            jax.ShapeDtypeStruct((8, ROWS), F32),
            jax.ShapeDtypeStruct((LOCAL, EMB, ROWS), BF16),
        ),
        in_specs=[hbm] * 7,
        out_specs=(vmem,) * 5,
        scratch_shapes=[
            pltpu.VMEM((FEAT, HID), BF16),
            pltpu.VMEM((ROWS, FEAT), BF16),
            pltpu.VMEM((SLOTS, RB, EMB), BF16),
            pltpu.VMEM((NC, RB, EMB), BF16),
            pltpu.VMEM((NC, RB, EMB), BF16),
            pltpu.VMEM((ROWS, HID), BF16),
            pltpu.VMEM((TAB, EMB, ROWS), BF16),
            pltpu.VMEM((NT, TAB, EB, ROWS), BF16),
            pltpu.VMEM((TAB + 1, EB, ROWS), BF16),
            pltpu.VMEM((SLOTS, EB, ROWS), BF16),
            pltpu.VMEM((1, ROWS), F32),
            pltpu.VMEM((NT, 1, ROWS), F32),
            pltpu.VMEM((1, ROWS), F32),
            pltpu.VMEM((NT, 1, ROWS), F32),
            pltpu.VMEM((1, ROWS), F32),
            pltpu.VMEM((NC, 1, ROWS), F32),
            pltpu.VMEM((1, HID), BF16),
            pltpu.VMEM((1, HID), BF16),
            pltpu.VMEM((1, ROWS), jnp.int32),
            pltpu.SMEM((TAB,), jnp.int32),
            pltpu.SMEM((NC,), jnp.int32),
            pltpu.VMEM((SLOTS, EMB), jnp.int32),
            pltpu.SMEM((SLOTS, EMB), jnp.int32),
            dma((6,)), dma,
            dma((NT,)), dma,
            tree, tree,
            dma((TAB,)), dma,
            dma((NC,)), dma,
            tree, tree,
            dma((NT,)), dma,
            dma((NT,)), dma,
            dma((NC,)), dma,
            dma((NT,)), dma,
            dma((NT,)), dma,
        ],
        compiler_params=pltpu.CompilerParams(
            collective_id=0, has_side_effects=True, vmem_limit_bytes=40 * 1024 * 1024
        ),
    )(
        slot_of_table, partner, labels.reshape(1, ROWS), jnp.transpose(pooled, (1, 0, 2)),
        w_first.reshape(FEAT, HID), b_first, w_head,
    )
    pg, gf, gb, gh, loss = pl.pallas_call(
        finish,
        out_shape=(
            jax.ShapeDtypeStruct((LOCAL, EMB, ROWS), BF16),
            jax.ShapeDtypeStruct((FEAT, HID), BF16),
            jax.ShapeDtypeStruct((1, HID), F32),
            jax.ShapeDtypeStruct((1, HID), F32),
            jax.ShapeDtypeStruct((1,), F32),
        ),
        in_specs=[vmem] * 5,
        out_specs=(vmem, hbm, vmem, vmem, smem),
        scratch_shapes=[
            pltpu.VMEM((ROWS, HID), BF16),
            pltpu.VMEM((FEAT, HID), BF16),
            dma((NCHUNK,)),
        ],
        compiler_params=pltpu.CompilerParams(vmem_limit_bytes=40 * 1024 * 1024),
    )(feat, act, a32, lg, sums)
    return pg, gf[None], gb, gh, loss


def solution(mesh):
    in_specs = (
        P("copy", "table", None), P(), P(), P("copy"), P("copy", None, "table"), P("copy", "table"), P("copy", "table"),
    )
    out_specs = (
        P("table", None, "copy"), P("copy", None, "table"), P("copy", "table"), P("copy", "table"), P("copy"),
    )
    return jax.shard_map(on_device, mesh=mesh, in_specs=in_specs, out_specs=out_specs, check_vma=False)
```

time: 129 us -> 104 us (0.81)
  Pallas kernels: 118 us -> 97 us
  between operations: 2.4 us -> 0.66 us
  local copies, waits for them, and re-layouts: 7.95 us -> 6.28 us
    pallas_call x1 -> x2, Pallas kernels: 118 us -> 97 us  [the longest x1 92 us: on_device(): pl.pallas_call(kernel, out_shape=(jax.ShapeDtypeStruct((ROWS, FEAT), BF16...]
    unnamed x16 -> x14, local copies, waits for them, and re-layouts: 7.95 us -> 6.28 us
where the time goes in v2:
time: 104 us
  Pallas kernels  97 us (93%)
  local copies, waits for them, and re-layouts  6.28 us (6%)
    pallas_call x1, Pallas kernels, on_device(): pl.pallas_call(kernel, out_shape=(jax.ShapeDtypeStruct((ROWS, FEAT), BF16...  92 us
    unnamed x14, local copies, waits for them, and re-layouts  6.28 us
    pallas_call x1, Pallas kernels, on_device(): pl.pallas_call(finish, out_shape=(jax.ShapeDtypeStruct((LOCAL, EMB, ROWS)...  5.01 us

profile of v2, /device:TPU:1, one launch (start us, length us, event | category | flops | bytes accessed | tf_op | source)
XLA Modules:
  0.0 103.9 jit_solution(13731530586576567345)
XLA Ops:
  0.6 0.0 copy-start
  0.6 2.0 %copy-done = bf16[1,3328,512]{2,1,0:T(8,128)(2,1)S(1)} copy-done((bf16[1,3328,512]{2,1,0:T(8,128)(2,1)S(1)}, bf16[1,3328,512]{2,1,0:T(8,128)(2,1)}, u32[]{:S(2)}) %copy-start) | copy-done | bytes 3407896
  2.6 0.0 copy-start.1
  2.6 1.0 copy-done.1
  3.6 0.0 copy-start.2
  3.6 0.7 copy-done.2
  4.3 0.0 copy-start.3
  4.3 0.7 copy-done.3
  4.9 0.0 copy-start.4
  4.9 0.7 copy-done.4
  5.6 0.0 copy-start.5
  5.6 0.7 copy-done.5
  6.3 0.0 copy-start.6
  6.3 0.7 copy-done.6
  6.9 92.0 %shard_map.110 = (bf16[256,3328]{1,0:T(8,128)(2,1)S(1)}, f32[256,512]{1,0:T(8,128)S(1)}, f32[256,512]{1,0:T(8,128)S(1)}, f32[8,256]{1,0:T(8,128)S(1)}, bf16[5,128,256]{2,1,0:T(8,128)(2,1)S(1)}) custom-call(s32[26]{0:T(128)S(1)} %copy-done.5, s32[32]{0:T(128)S(1)} %copy-done.6, s32[1,256]{1,0:T(1,128)S(1)} %bitcast.6, bf16[5,256,128]{2,1,0:T(8,128)(2,1)S(1)} %bitcast.5, ...), custom_call_target="tpu_custom_call" | custom-call | tf_op jit(solution)/shard_map/pallas_call | solution.py:381
  98.9 5.0 %shard_map.111 = (bf16[5,128,256]{2,1,0:T(8,128)(2,1)}, bf16[3328,512]{1,0:T(8,128)(2,1)}, f32[1,512]{1,0:T(1,128)}, f32[1,512]{1,0:T(1,128)}, f32[1]{0:T(128)}) custom-call(bf16[256,3328]{1,0:T(8,128)(2,1)S(1)} %get-tuple-element.15.feat, f32[256,512]{1,0:T(8,128)S(1)} %get-tuple-element.16.act_v, f32[256,512]{1,0:T(8,128)S(1)} %get-tuple-element.17.a32_v, ...), custom_call_target="tpu_custom_call" | custom-call | tf_op jit(solution)/shard_map/pallas_call | solution.py:435
Async XLA Ops:
  0.6 2.0 %copy-start = (bf16[1,3328,512]{2,1,0:T(8,128)(2,1)S(1)}, bf16[1,3328,512]{2,1,0:T(8,128)(2,1)}, u32[]{:S(2)}) copy-start(bf16[1,3328,512]{2,1,0:T(8,128)(2,1)} %param.11) | copy-start | bytes 10223620
  2.6 1.0 copy-start.1
  3.6 0.7 copy-start.2
  4.3 0.7 copy-start.3
  4.9 0.7 copy-start.4
  5.6 0.7 copy-start.5
  6.3 0.7 copy-start.6

commit v3 on v2

--- a/solution.py
+++ b/solution.py
@@ -43,8 +43,9 @@
 
 def kernel(
     slot_h, partner_h, labels_h, pooled, w_hbm, b_h, h_h,
-    feat, act_v, a32_v, lg_out, pg_out,
-    w_v, feat_t, by_slot, relay_in, relay_out, low_v, gt_v, part_in, sums, placed,
+    gf_v, pg_out, gb_out, gh_out, loss_out,
+    w_v, feat, feat_t, by_slot, relay_in, relay_out, act_v, a32_v, low_v, gt_v, in_b, in_a1, in_a2, in_low, in_high, in_al, in_ar,
+    in_ay, in_l, in_r, sums, placed, pg_in,
     z_own, z_in, q_own, q_in, qs_own, qs_in, b_v, h_v, y_v, slot_s, partner_s, inv_v, inv_s,
     load_sem, inv_sem,
     a_send, a_recv, ag_send, ag_recv, c_send, c_recv, d_send, d_recv, tg_send, tg_recv,
@@ -209,6 +210,16 @@
         total = total + (weighed[:, :EMB] + weighed[:, EMB:])
     z_own[...] = head_row(total)
 
+    z_in[k] = z_own[...]
+
+    def l_copy(d, j):
+        return remote(z_own, z_in.at[k], l_send.at[d], l_recv, c, j)
+
+    over_table(lambda d, j: l_copy(d, j).start())
+
+    take(feat_t.at[my_rows], d_recv)
+    tree_step(feat_t, tg_send, tg_recv, 0)
+
     def gt_step(i, _):
         rows = pl.ds(pl.multiple_of(i * CH, CH), CH)
         g = lax.dot_general(w_v[rows, :], low_v[...], (((1,), (1,)), ((), ())), preferred_element_type=F32)
@@ -217,51 +228,42 @@
 
     lax.fori_loop(0, NCHUNK, gt_step, 0)
 
-    z_in[k] = z_own[...]
-
-    def l_copy(d, j):
-        return remote(z_own, z_in.at[k], l_send.at[d], l_recv, c, j)
-
-    over_table(lambda d, j: l_copy(d, j).start())
-
-    def r_copy(d, j):
-        part = pl.ds(pl.multiple_of(j * EB, EB), EB)
-        return remote(gt_v.at[:, part, :], part_in.at[k], r_send.at[d], r_recv, c, j)
-
-    over_table(lambda d, j: r_copy(d, j).start())
-    my_part = pl.ds(pl.multiple_of(k * EB, EB), EB)
-    pltpu.make_async_copy(gt_v.at[:, my_part, :], part_in.at[k], r_recv).start()
-
-    take(feat_t.at[my_rows], d_recv)
-    tree_step(feat_t, tg_send, tg_recv, 0)
-
-    take(part_in, r_recv)
-    inv_copy.wait()
-    sums[TAB] = jnp.zeros((EB, ROWS), BF16)
-
-    def sum_step(t, _):
-        total = part_in[0, t].astype(F32)
-        for j in range(1, NT):
-            total = total + part_in[j, t].astype(F32)
-        sums[t] = total.astype(BF16)
-        return 0
-
-    lax.fori_loop(0, TAB, sum_step, 0, unroll=2)
-
-    def place(s, _):
-        placed[s] = sums[inv_s[s, 0]]
-        return 0
-
-    lax.fori_loop(0, SLOTS, place, 0, unroll=4)
-
-    def z_copy(d, j):
-        return remote(placed.at[pl.ds(j * LOCAL, LOCAL)], pg_out.at[:, my_part, :], z_send.at[d], z_recv, c, j)
-
-    over_table(lambda d, j: z_copy(d, j).start())
-    pltpu.make_async_copy(placed.at[pl.ds(k * LOCAL, LOCAL)], pg_out.at[:, my_part, :], z_recv).start()
-
-    for step in range(1, len(TREE_STEPS)):
+    for step in range(1, 7):
         tree_step(feat_t, tg_send, tg_recv, step)
+
+    def part(step, tables=(0, TAB), lanes=(0, ROWS)):
+        first = pl.multiple_of(share(step) * EB, EB)
+        return pl.ds(tables[0], tables[1]), pl.ds(first, EB), pl.ds(lanes[0], lanes[1])
+
+    ta, tb = (0, TAB // 2), (TAB // 2, TAB // 2)
+    low, high = (0, EMB), (EMB, EMB)
+    sends = []
+
+    def reduce_send(step, tables, lanes, dst, to):
+        i = len(sends)
+        where = part(step, tables, lanes)
+        copy = remote(gt_v.at[where], dst, r_send.at[i], r_recv.at[i], c, target[to])
+        copy.start()
+        sends.append(copy)
+
+    def add(step, tables, lanes, *arrived):
+        where = part(step, tables, lanes)
+        total = gt_v[where].astype(F32)
+        for ref, i in arrived:
+            take(ref, r_recv.at[i])
+            total = total + ref[...].astype(F32)
+        gt_v[where] = total.astype(BF16)
+
+    full = (0, ROWS)
+    every = (0, TAB)
+    reduce_send((2, 1), tb, full, in_b.at[0], "y")
+    reduce_send((2, 1), ta, low, in_a1, "left")
+    reduce_send((2, 1), ta, high, in_a2, "right")
+    reduce_send((3, 1), tb, full, in_b.at[1], "y")
+    reduce_send((1, 1), tb, full, in_b.at[2], "y")
+    reduce_send((0, 1), tb, full, in_b.at[3], "y")
+
+    tree_step(feat_t, tg_send, tg_recv, 7)
     total = jnp.zeros((ROWS, EMB), F32)
     for n in range(HID // CH):
         cols = slice(n * CH, (n + 1) * CH)
@@ -275,6 +277,15 @@
         return remote(q_own, q_in.at[k], m_send.at[d], m_recv, c, j)
 
     over_table(lambda d, j: m_copy(d, j).start())
+
+    add((2, 0), tb, full, (in_b.at[0], 0))
+    reduce_send((2, 0), every, low, in_low, "left")
+    reduce_send((2, 0), every, high, in_high, "right")
+    add((3, 1), ta, low, (in_a1, 1))
+    reduce_send((3, 1), ta, full, in_al, "left")
+    add((1, 1), ta, high, (in_a2, 2))
+    reduce_send((1, 1), ta, full, in_ar, "right")
+
     take(z_in.at[pl.ds(0, NT - 1)], l_recv)
     take(q_in.at[pl.ds(0, NT - 1)], m_recv)
     qs_own[...] = jnp.sum(q_in[...], axis=0)
@@ -288,59 +299,25 @@
         return 0
 
     lax.fori_loop(1, NC, t_start, 0)
+
+    add((3, 0), tb, full, (in_b.at[1], 3))
+    add((3, 0), every, low, (in_low, 6))
+    reduce_send((3, 0), every, full, in_l, "left")
+    add((1, 0), tb, full, (in_b.at[2], 4))
+    add((1, 0), every, high, (in_high, 7))
+    reduce_send((1, 0), every, full, in_r, "right")
+    add((0, 1), ta, full, (in_al, 8), (in_ar, 9))
+    reduce_send((0, 1), ta, full, in_ay, "y")
+
     take(qs_in.at[pl.ds(0, NC - 1)], t_recv)
-
     z = jnp.sum(z_in[...], axis=0)
     q = jax.nn.sigmoid(qs_in[partner_s[c]])
     target_y = y_v[...].astype(F32)
     soft = jnp.maximum(z, 0.0) + jnp.log1p(jnp.exp(-jnp.abs(z)))
-    lg_out[...] = jnp.zeros_like(lg_out)
-    lg_out[0:1, :] = 2.0 * jax.nn.sigmoid(z) - target_y - q
-    lg_out[1:2, :] = 2.0 * soft - target_y * z - q * z
-
-    take(pg_out, z_recv)
-
-    over_table(lambda d, j: a_copy(d, j).wait_send())
-
-    def c_wait(i, _):
-        _, to, copy = c_copy(i)
-
-        @pl.when(to != c)
-        def _():
-            copy.wait_send()
-
-        return 0
-
-    lax.fori_loop(0, TAB, c_wait, 0)
-    for i in range(len(TREE)):
-        tree_copy(feat, ag_send, ag_recv, i).wait_send()
-        tree_copy(feat_t, tg_send, tg_recv, i).wait_send()
-
-    @pl.when(is_relay)
-    def _():
-        def d_wait(d, _):
-            d_copy(d, lax.rem(c + d, NC)).wait_send()
-            return 0
-
-        lax.fori_loop(1, NC, d_wait, 0)
-
-    def t_wait(d, _):
-        t_copy(d).wait_send()
-        return 0
-
-    lax.fori_loop(1, NC, t_wait, 0)
-
-    def rest(d, j):
-        l_copy(d, j).wait_send()
-        m_copy(d, j).wait_send()
-        r_copy(d, j).wait_send()
-        z_copy(d, j).wait_send()
-
-    over_table(rest)
-
-
-def finish(feat, act_v, a32_v, lg_v, pg_v, pg_out, gf_out, gb_out, gh_out, loss_out, low_v, gf_v, gf_sem):
-    lg = lg_v[0:1, :]
+    lg = 2.0 * jax.nn.sigmoid(z) - target_y - q
+    loss_out[...] = jnp.broadcast_to(
+        jnp.sum(2.0 * soft - target_y * z - q * z, axis=1, keepdims=True) * (1.0 / ROWS), (1, EMB)
+    )
     lg_col = jnp.transpose(jnp.broadcast_to(lg, (EMB, ROWS)))
     for n in range(HID // EMB):
         cols = slice(n * EMB, (n + 1) * EMB)
@@ -349,27 +326,90 @@
         gb_out[:, cols] = jnp.sum(grad_pre, axis=0, keepdims=True)
         gh_out[:, cols] = jnp.sum(lg_col * act_v[:, cols], axis=0, keepdims=True)
 
-    def gf_copy(i):
-        rows = pl.ds(pl.multiple_of(i * CH, CH), CH)
-        return pltpu.make_async_copy(gf_v.at[rows], gf_out.at[rows], gf_sem.at[i])
+    for ref, i in ((in_b.at[3], 5), (in_l, 10), (in_r, 11), (in_ay, 12)):
+        take(ref, r_recv.at[i])
+    inv_copy.wait()
+    mine = pl.ds(pl.multiple_of(k * EB, EB), EB)
+    half = TAB // 2
+    total = gt_v[0:half, mine, :].astype(F32) + in_ay[...].astype(F32)
+    total = total + in_l[0:half].astype(F32) + in_r[0:half].astype(F32)
+    sums[0:half] = (total * lg[None]).astype(BF16)
+    total = gt_v[half:TAB, mine, :].astype(F32) + in_b[3].astype(F32)
+    total = total + in_l[half:TAB].astype(F32) + in_r[half:TAB].astype(F32)
+    sums[half:TAB] = (total * lg[None]).astype(BF16)
+    sums[TAB] = jnp.zeros((EB, ROWS), BF16)
+
+    def place(s, _):
+        placed[s] = sums[inv_s[s, 0]]
+        return 0
+
+    lax.fori_loop(0, SLOTS, place, 0, unroll=4)
+
+    def z_copy(d, j):
+        return remote(placed.at[pl.ds(j * LOCAL, LOCAL)], pg_in.at[:, mine, :], z_send.at[d], z_recv, c, j)
+
+    over_table(lambda d, j: z_copy(d, j).start())
+    pltpu.make_async_copy(placed.at[pl.ds(k * LOCAL, LOCAL)], pg_in.at[:, mine, :], z_recv).start()
 
     def gf_step(i, _):
         rows = pl.ds(pl.multiple_of(i * CH, CH), CH)
         g = lax.dot_general(feat[:, rows], low_v[...], (((0,), (0,)), ((), ())), preferred_element_type=F32)
         gf_v[rows, :] = g.astype(BF16)
-        gf_copy(i).start()
         return 0
 
     lax.fori_loop(0, NCHUNK, gf_step, 0)
-    loss_out[0] = jnp.sum(lg_v[1:2, :]) * (1.0 / ROWS)
-    for s in range(LOCAL):
-        pg_out[s] = (pg_v[s].astype(F32) * lg).astype(BF16)
-
-    def gf_wait(i, _):
-        gf_copy(i).wait()
-        return 0
-
-    lax.fori_loop(0, NCHUNK, gf_wait, 0)
+
+    over_table(lambda d, j: a_copy(d, j).wait_send())
+
+    def c_wait(i, _):
+        _, to, copy = c_copy(i)
+
+        @pl.when(to != c)
+        def _():
+            copy.wait_send()
+
+        return 0
+
+    lax.fori_loop(0, TAB, c_wait, 0)
+    for i in range(len(TREE)):
+        tree_copy(feat, ag_send, ag_recv, i).wait_send()
+        tree_copy(feat_t, tg_send, tg_recv, i).wait_send()
+
+    @pl.when(is_relay)
+    def _():
+        def d_wait(d, _):
+            d_copy(d, lax.rem(c + d, NC)).wait_send()
+            return 0
+
+        lax.fori_loop(1, NC, d_wait, 0)
+
+    def t_wait(d, _):
+        t_copy(d).wait_send()
+        return 0
+
+    lax.fori_loop(1, NC, t_wait, 0)
+
+    def rest(d, j):
+        l_copy(d, j).wait_send()
+        m_copy(d, j).wait_send()
+        z_copy(d, j).wait_send()
+
+    over_table(rest)
+    for copy in sends:
+        copy.wait_send()
+    take(pg_in, z_recv)
+    pg_out[...] = pg_in[...]
+
+
+def finish(gf_v, pg_v, gb_v, gh_v, loss_v, pg_out, gf_out, gb_out, gh_out, loss_out, sem):
+    copies = [pltpu.make_async_copy(gf_v, gf_out, sem.at[0]), pltpu.make_async_copy(pg_v, pg_out, sem.at[1])]
+    for copy in copies:
+        copy.start()
+    gb_out[...] = gb_v[...]
+    gh_out[...] = gh_v[...]
+    loss_out[0] = jnp.sum(loss_v[:, 0:1])
+    for copy in copies:
+        copy.wait()
 
 
 def on_device(pooled, slot_of_table, partner, labels, w_first, b_first, w_head):
@@ -378,28 +418,41 @@
     hbm = pl.BlockSpec(memory_space=pltpu.HBM)
     dma = pltpu.SemaphoreType.DMA
     tree = dma((len(TREE),))
-    feat, act, a32, lg, sums = pl.pallas_call(
+    results = pl.pallas_call(
         kernel,
         out_shape=(
-            jax.ShapeDtypeStruct((ROWS, FEAT), BF16),
-            jax.ShapeDtypeStruct((ROWS, HID), F32),
-            jax.ShapeDtypeStruct((ROWS, HID), F32),
-            jax.ShapeDtypeStruct((8, ROWS), F32),
+            jax.ShapeDtypeStruct((FEAT, HID), BF16),
             jax.ShapeDtypeStruct((LOCAL, EMB, ROWS), BF16),
+            jax.ShapeDtypeStruct((1, HID), F32),
+            jax.ShapeDtypeStruct((1, HID), F32),
+            jax.ShapeDtypeStruct((1, EMB), F32),
         ),
         in_specs=[hbm] * 7,
         out_specs=(vmem,) * 5,
         scratch_shapes=[
             pltpu.VMEM((FEAT, HID), BF16),
             pltpu.VMEM((ROWS, FEAT), BF16),
+            pltpu.VMEM((ROWS, FEAT), BF16),
             pltpu.VMEM((SLOTS, RB, EMB), BF16),
             pltpu.VMEM((NC, RB, EMB), BF16),
             pltpu.VMEM((NC, RB, EMB), BF16),
+            pltpu.VMEM((ROWS, HID), F32),
+            pltpu.VMEM((ROWS, HID), F32),
             pltpu.VMEM((ROWS, HID), BF16),
             pltpu.VMEM((TAB, EMB, ROWS), BF16),
-            pltpu.VMEM((NT, TAB, EB, ROWS), BF16),
+            pltpu.VMEM((4, TAB // 2, EB, ROWS), BF16),
+            pltpu.VMEM((TAB // 2, EB, EMB), BF16),
+            pltpu.VMEM((TAB // 2, EB, EMB), BF16),
+            pltpu.VMEM((TAB, EB, EMB), BF16),
+            pltpu.VMEM((TAB, EB, EMB), BF16),
+            pltpu.VMEM((TAB // 2, EB, ROWS), BF16),
+            pltpu.VMEM((TAB // 2, EB, ROWS), BF16),
+            pltpu.VMEM((TAB // 2, EB, ROWS), BF16),
+            pltpu.VMEM((TAB, EB, ROWS), BF16),
+            pltpu.VMEM((TAB, EB, ROWS), BF16),
             pltpu.VMEM((TAB + 1, EB, ROWS), BF16),
             pltpu.VMEM((SLOTS, EB, ROWS), BF16),
+            pltpu.VMEM((LOCAL, EMB, ROWS), BF16),
             pltpu.VMEM((1, ROWS), F32),
             pltpu.VMEM((NT, 1, ROWS), F32),
             pltpu.VMEM((1, ROWS), F32),
@@ -422,15 +475,20 @@
             dma((NT,)), dma,
             dma((NT,)), dma,
             dma((NC,)), dma,
-            dma((NT,)), dma,
+            tree, tree,
             dma((NT,)), dma,
         ],
         compiler_params=pltpu.CompilerParams(
             collective_id=0, has_side_effects=True, vmem_limit_bytes=40 * 1024 * 1024
         ),
     )(
-        slot_of_table, partner, labels.reshape(1, ROWS), jnp.transpose(pooled, (1, 0, 2)),
-        w_first.reshape(FEAT, HID), b_first, w_head,
+        *(
+            pltpu.with_memory_space_constraint(v, pltpu.HBM)
+            for v in (
+                slot_of_table, partner, labels.reshape(1, ROWS), jnp.transpose(pooled, (1, 0, 2)),
+                w_first.reshape(FEAT, HID), b_first, w_head,
+            )
+        )
     )
     pg, gf, gb, gh, loss = pl.pallas_call(
         finish,
@@ -442,14 +500,10 @@
             jax.ShapeDtypeStruct((1,), F32),
         ),
         in_specs=[vmem] * 5,
-        out_specs=(vmem, hbm, vmem, vmem, smem),
-        scratch_shapes=[
-            pltpu.VMEM((ROWS, HID), BF16),
-            pltpu.VMEM((FEAT, HID), BF16),
-            dma((NCHUNK,)),
-        ],
-        compiler_params=pltpu.CompilerParams(vmem_limit_bytes=40 * 1024 * 1024),
-    )(feat, act, a32, lg, sums)
+        out_specs=(hbm, hbm, vmem, vmem, smem),
+        scratch_shapes=[dma((2,))],
+        compiler_params=pltpu.CompilerParams(vmem_limit_bytes=24 * 1024 * 1024),
+    )(*results)
     return pg, gf[None], gb, gh, loss
 
 

time: 104 us -> 81.7 us (0.79)
  Pallas kernels: 97 us -> 81 us
  local copies, waits for them, and re-layouts: 6.28 us -> 0 us
    pallas_call x1, Pallas kernels: 92 us -> 78.6 us  [on_device(): pl.pallas_call(kernel, out_shape=(jax.ShapeDtypeStruct((FEAT, HID), BF16)...]
    unnamed x14 -> x0, local copies, waits for them, and re-layouts: 6.28 us -> none
    pallas_call x1, Pallas kernels: 5.01 us -> 2.46 us  [on_device(): pl.pallas_call(finish, out_shape=(jax.ShapeDtypeStruct((LOCAL, EMB, ROWS)...]
where the time goes in v3:
time: 81.7 us; the launch traced here: 81.6 us
  Pallas kernels  81 us (99%)
    pallas_call x1, Pallas kernels, on_device(): pl.pallas_call(kernel, out_shape=(jax.ShapeDtypeStruct((FEAT, HID), BF16)...  78.6 us
    pallas_call x1, Pallas kernels, on_device(): pl.pallas_call(finish, out_shape=(jax.ShapeDtypeStruct((LOCAL, EMB, ROWS)...  2.46 us

profile of v3, /device:TPU:1, one launch (start us, length us, event | category | flops | bytes accessed | tf_op | source)
XLA Modules:
  0.0 81.6 jit_solution(5763729470204762732)
XLA Ops:
  0.6 78.6 %shard_map.110 = (bf16[3328,512]{1,0:T(8,128)(2,1)S(1)}, bf16[5,128,256]{2,1,0:T(8,128)(2,1)S(1)}, f32[1,512]{1,0:T(1,128)S(1)}, f32[1,512]{1,0:T(1,128)S(1)}, f32[1,128]{1,0:T(1,128)S(1)}) custom-call(s32[26]{0:T(128)} %slot_h.1, s32[32]{0:T(128)} %partner_h.1, s32[1,256]{1,0:T(1,128)} %bitcast.6, bf16[5,256,128]{2,1,0:T(8,128)(2,1)} %bitcast.5, ...), custom_call_target="tpu_custom_call" | custom-call | tf_op jit(solution)/shard_map/pallas_call | solution.py:421
  79.2 2.5 %shard_map.111 = (bf16[5,128,256]{2,1,0:T(8,128)(2,1)}, bf16[3328,512]{1,0:T(8,128)(2,1)}, f32[1,512]{1,0:T(1,128)}, f32[1,512]{1,0:T(1,128)}, f32[1]{0:T(128)}) custom-call(bf16[3328,512]{1,0:T(8,128)(2,1)S(1)} %get-tuple-element.15.gf_v, bf16[5,128,256]{2,1,0:T(8,128)(2,1)S(1)} %get-tuple-element.16.pg_v, f32[1,512]{1,0:T(1,128)S(1)} %get-tuple-element.17.gb_v, ...), custom_call_target="tpu_custom_call" | custom-call | tf_op jit(solution)/shard_map/pallas_call | solution.py:493

commit v4 on v3

--- a/solution.py
+++ b/solution.py
@@ -47,7 +47,7 @@
     w_v, feat, feat_t, by_slot, relay_in, relay_out, act_v, a32_v, low_v, gt_v, in_b, in_a1, in_a2, in_low, in_high, in_al, in_ar,
     in_ay, in_l, in_r, sums, placed, pg_in,
     z_own, z_in, q_own, q_in, qs_own, qs_in, b_v, h_v, y_v, slot_s, partner_s, inv_v, inv_s,
-    load_sem, inv_sem,
+    in_sem, go_sem, load_sem, inv_sem,
     a_send, a_recv, ag_send, ag_recv, c_send, c_recv, d_send, d_recv, tg_send, tg_recv,
     l_send, l_recv, m_send, m_recv, t_send, t_recv, r_send, r_recv, z_send, z_recv,
 ):
@@ -61,16 +61,21 @@
 
     barrier = pltpu.get_barrier_semaphore()
 
+    is_gate = k == 0
+
+    def signal(sem, copy, table):
+        pl.semaphore_signal(sem, inc=1, device_id=(copy, table), device_id_type=MESH)
+
     def greet_table(d, _):
-        pl.semaphore_signal(barrier, inc=1, device_id=(c, lax.rem(k + d, NT)), device_id_type=MESH)
-        return 0
-
-    def greet_copy(d, _):
-        pl.semaphore_signal(barrier, inc=1, device_id=(lax.rem(c + d, NC), k), device_id_type=MESH)
+        j = lax.rem(k + d, NT)
+
+        @pl.when(j != 0)
+        def _():
+            signal(barrier, c, j)
+
         return 0
 
     lax.fori_loop(1, NT, greet_table, 0)
-    lax.fori_loop(1, NC, greet_copy, 0)
 
     loads = [
         pltpu.make_async_copy(src, dst, load_sem.at[i])
@@ -80,7 +85,32 @@
     ]
     for load in loads:
         load.start()
-    pl.semaphore_wait(barrier, NT - 1 + NC - 1)
+
+    @pl.when(jnp.logical_not(is_gate))
+    def _():
+        pl.semaphore_wait(barrier, NT - 1)
+        signal(in_sem, c, 0)
+
+    @pl.when(is_gate)
+    def _():
+        pl.semaphore_wait(in_sem, NT - 1)
+
+        def greet_copy(d, _):
+            signal(barrier, lax.rem(c + d, NC), k)
+            return 0
+
+        lax.fori_loop(1, NC, greet_copy, 0)
+
+    def all_in():
+        @pl.when(is_gate)
+        def _():
+            pl.semaphore_wait(barrier, NC - 1)
+            for j in range(1, NT):
+                signal(go_sem, c, j)
+
+        @pl.when(jnp.logical_not(is_gate))
+        def _():
+            pl.semaphore_wait(go_sem, 1)
 
     def remote(src, dst, send, recv, copy, table):
         return pltpu.make_async_remote_copy(
@@ -163,6 +193,7 @@
 
         return 0
 
+    all_in()
     lax.fori_loop(0, TAB, c_start, 0)
     for step in range(1, 6):
         tree_step(feat, ag_send, ag_recv, step)
@@ -466,6 +497,7 @@
             pltpu.SMEM((NC,), jnp.int32),
             pltpu.VMEM((SLOTS, EMB), jnp.int32),
             pltpu.SMEM((SLOTS, EMB), jnp.int32),
+            pltpu.SemaphoreType.REGULAR, pltpu.SemaphoreType.REGULAR,
             dma((6,)), dma,
             dma((NT,)), dma,
             tree, tree,

time: 81.7 us -> 79.5 us (0.973)
  Pallas kernels: 81 us -> 78.8 us
    pallas_call x1, Pallas kernels: 78.6 us -> 76.3 us  [on_device(): pl.pallas_call(kernel, out_shape=(jax.ShapeDtypeStruct((FEAT, HID), BF16)...]
where the time goes in v4:
time: 79.5 us; the launch traced here: 79.4 us
  Pallas kernels  78.8 us (99%)
    pallas_call x1, Pallas kernels, on_device(): pl.pallas_call(kernel, out_shape=(jax.ShapeDtypeStruct((FEAT, HID), BF16)...  76.3 us
    pallas_call x1, Pallas kernels, on_device(): pl.pallas_call(finish, out_shape=(jax.ShapeDtypeStruct((LOCAL, EMB, ROWS)...  2.46 us

profile of v4, /device:TPU:1, one launch (start us, length us, event | category | flops | bytes accessed | tf_op | source)
XLA Modules:
  0.0 79.4 jit_solution(12431519405666523125)
XLA Ops:
  0.6 76.3 %shard_map.110 = (bf16[3328,512]{1,0:T(8,128)(2,1)S(1)}, bf16[5,128,256]{2,1,0:T(8,128)(2,1)S(1)}, f32[1,512]{1,0:T(1,128)S(1)}, f32[1,512]{1,0:T(1,128)S(1)}, f32[1,128]{1,0:T(1,128)S(1)}) custom-call(s32[26]{0:T(128)} %slot_h.1, s32[32]{0:T(128)} %partner_h.1, s32[1,256]{1,0:T(1,128)} %bitcast.6, bf16[5,256,128]{2,1,0:T(8,128)(2,1)} %bitcast.5, ...), custom_call_target="tpu_custom_call" | custom-call | tf_op jit(solution)/shard_map/pallas_call | solution.py:452
  77.0 2.5 %shard_map.111 = (bf16[5,128,256]{2,1,0:T(8,128)(2,1)}, bf16[3328,512]{1,0:T(8,128)(2,1)}, f32[1,512]{1,0:T(1,128)}, f32[1,512]{1,0:T(1,128)}, f32[1]{0:T(128)}) custom-call(bf16[3328,512]{1,0:T(8,128)(2,1)S(1)} %get-tuple-element.15.gf_v, bf16[5,128,256]{2,1,0:T(8,128)(2,1)S(1)} %get-tuple-element.16.pg_v, f32[1,512]{1,0:T(1,128)S(1)} %get-tuple-element.17.gb_v, ...), custom_call_target="tpu_custom_call" | custom-call | tf_op jit(solution)/shard_map/pallas_call | solution.py:525

commit v5 on v4

--- a/solution.py
+++ b/solution.py
@@ -37,13 +37,13 @@
               ((1, 8, 9, 10, 11, 12), ()))
 
 
-def relay_copy(t):
-    return jnp.where(t < 24, (t // 3) * 4 + t % 3, jnp.where(t == 24, 3, 19))
+def relay_copy(r):
+    return 2 * (r + jnp.where(r >= 5, 1, 0) + jnp.where(r >= 9, 1, 0))
 
 
 def kernel(
     slot_h, partner_h, labels_h, pooled, w_hbm, b_h, h_h,
-    gf_v, pg_out, gb_out, gh_out, loss_out,
+    ft_out, low_out, pg_out, gb_out, gh_out, loss_out,
     w_v, feat, feat_t, by_slot, relay_in, relay_out, act_v, a32_v, low_v, gt_v, in_b, in_a1, in_a2, in_low, in_high, in_al, in_ar,
     in_ay, in_l, in_r, sums, placed, pg_in,
     z_own, z_in, q_own, q_in, qs_own, qs_in, b_v, h_v, y_v, slot_s, partner_s, inv_v, inv_s,
@@ -55,9 +55,9 @@
     k = lax.axis_index("table")
     x, y = lax.rem(k, 4), k // 4
     my_rows = pl.ds(pl.multiple_of(k * RB, RB), RB)
-    zq = lax.rem(c, 4)
-    my_t = jnp.where(zq < 3, (c // 4) * 3 + zq, jnp.where(c == 3, 24, 25))
-    is_relay = jnp.logical_or(zq < 3, jnp.logical_or(c == 3, c == 19))
+    chip = c // 2
+    is_relay = (lax.rem(c, 2) == 0) & (chip != 5) & (chip != 10) & (chip != 15)
+    my_r = jnp.where(is_relay, chip - jnp.where(chip >= 5, 1, 0) - jnp.where(chip >= 10, 1, 0), 0)
 
     barrier = pltpu.get_barrier_semaphore()
 
@@ -175,9 +175,9 @@
     tree_step(feat, ag_send, ag_recv, 0)
 
     def c_copy(i):
-        t = lax.rem(i + my_t, TAB)
-        to = relay_copy(t)
-        src = feat.at[my_rows, pl.ds(pl.multiple_of(t * EMB, EMB), EMB)]
+        r = lax.rem(i + my_r, NCHUNK)
+        to = relay_copy(r)
+        src = feat.at[my_rows, pl.ds(pl.multiple_of(r * CH, CH), CH)]
         return src, to, remote(src, relay_in.at[c], c_send.at[i], c_recv, to, k)
 
     def c_start(i, _):
@@ -194,11 +194,11 @@
         return 0
 
     all_in()
-    lax.fori_loop(0, TAB, c_start, 0)
+    lax.fori_loop(0, NCHUNK, c_start, 0)
     for step in range(1, 6):
         tree_step(feat, ag_send, ag_recv, step)
 
-    my_cols = pl.ds(pl.multiple_of(my_t * EMB, EMB), EMB)
+    my_cols = pl.ds(pl.multiple_of(my_r * CH, CH), CH)
 
     def d_copy(d, p):
         return remote(relay_out.at[p], feat_t.at[my_rows, my_cols], d_send.at[d], d_recv, p, k)
@@ -248,34 +248,40 @@
 
     over_table(lambda d, j: l_copy(d, j).start())
 
-    take(feat_t.at[my_rows], d_recv)
-    tree_step(feat_t, tg_send, tg_recv, 0)
-
-    def gt_step(i, _):
-        rows = pl.ds(pl.multiple_of(i * CH, CH), CH)
-        g = lax.dot_general(w_v[rows, :], low_v[...], (((1,), (1,)), ((), ())), preferred_element_type=F32)
-        gt_v[pl.ds(i * 2, 2)] = g.astype(BF16).reshape(2, EMB, ROWS)
-        return 0
-
-    lax.fori_loop(0, NCHUNK, gt_step, 0)
-
-    for step in range(1, 7):
-        tree_step(feat_t, tg_send, tg_recv, step)
+    def partials():
+        def gt_step(i, _):
+            rows = pl.ds(pl.multiple_of(i * CH, CH), CH)
+            g = lax.dot_general(w_v[rows, :], low_v[...], (((1,), (1,)), ((), ())), preferred_element_type=F32)
+            gt_v[pl.ds(i * 2, 2)] = g.astype(BF16).reshape(2, EMB, ROWS)
+            return 0
+
+        lax.fori_loop(0, NCHUNK, gt_step, 0)
 
     def part(step, tables=(0, TAB), lanes=(0, ROWS)):
         first = pl.multiple_of(share(step) * EB, EB)
         return pl.ds(tables[0], tables[1]), pl.ds(first, EB), pl.ds(lanes[0], lanes[1])
 
-    ta, tb = (0, TAB // 2), (TAB // 2, TAB // 2)
-    low, high = (0, EMB), (EMB, EMB)
-    sends = []
-
-    def reduce_send(step, tables, lanes, dst, to):
-        i = len(sends)
-        where = part(step, tables, lanes)
-        copy = remote(gt_v.at[where], dst, r_send.at[i], r_recv.at[i], c, target[to])
-        copy.start()
-        sends.append(copy)
+    ta, tb, every = (0, TAB // 2), (TAB // 2, TAB // 2), (0, TAB)
+    low, high, full = (0, EMB), (EMB, EMB), (0, ROWS)
+    messages = (
+        ((2, 1), tb, full, in_b.at[0], "y"),
+        ((2, 1), ta, low, in_a1, "left"),
+        ((2, 1), ta, high, in_a2, "right"),
+        ((3, 1), tb, full, in_b.at[1], "y"),
+        ((1, 1), tb, full, in_b.at[2], "y"),
+        ((0, 1), tb, full, in_b.at[3], "y"),
+        ((2, 0), every, low, in_low, "left"),
+        ((2, 0), every, high, in_high, "right"),
+        ((3, 1), ta, full, in_al, "left"),
+        ((1, 1), ta, full, in_ar, "right"),
+        ((3, 0), every, full, in_l, "left"),
+        ((1, 0), every, full, in_r, "right"),
+        ((0, 1), ta, full, in_ay, "y"),
+    )
+
+    def reduce_copy(i):
+        step, tables, lanes, dst, to = messages[i]
+        return remote(gt_v.at[part(step, tables, lanes)], dst, r_send.at[i], r_recv.at[i], c, target[to])
 
     def add(step, tables, lanes, *arrived):
         where = part(step, tables, lanes)
@@ -285,16 +291,62 @@
             total = total + ref[...].astype(F32)
         gt_v[where] = total.astype(BF16)
 
-    full = (0, ROWS)
-    every = (0, TAB)
-    reduce_send((2, 1), tb, full, in_b.at[0], "y")
-    reduce_send((2, 1), ta, low, in_a1, "left")
-    reduce_send((2, 1), ta, high, in_a2, "right")
-    reduce_send((3, 1), tb, full, in_b.at[1], "y")
-    reduce_send((1, 1), tb, full, in_b.at[2], "y")
-    reduce_send((0, 1), tb, full, in_b.at[3], "y")
+    def reduce_leaves():
+        for i in range(6):
+            reduce_copy(i).start()
+
+    def reduce_first():
+        add((2, 0), tb, full, (in_b.at[0], 0))
+        reduce_copy(6).start()
+        reduce_copy(7).start()
+        add((3, 1), ta, low, (in_a1, 1))
+        reduce_copy(8).start()
+        add((1, 1), ta, high, (in_a2, 2))
+        reduce_copy(9).start()
+
+    def reduce_second():
+        add((3, 0), tb, full, (in_b.at[1], 3))
+        add((3, 0), every, low, (in_low, 6))
+        reduce_copy(10).start()
+        add((1, 0), tb, full, (in_b.at[2], 4))
+        add((1, 0), every, high, (in_high, 7))
+        reduce_copy(11).start()
+        add((0, 1), ta, full, (in_al, 8), (in_ar, 9))
+        reduce_copy(12).start()
+
+    ahead = c < NC // 2
+    behind = jnp.logical_not(ahead)
+
+    @pl.when(ahead)
+    def _():
+        partials()
+        reduce_leaves()
+        reduce_first()
+
+    take(feat_t.at[my_rows], d_recv)
+    tree_step(feat_t, tg_send, tg_recv, 0)
+
+    @pl.when(behind)
+    def _():
+        partials()
+
+
+    for step in range(1, 7):
+        tree_step(feat_t, tg_send, tg_recv, step)
+
+    @pl.when(behind)
+    def _():
+        reduce_leaves()
+
+    @pl.when(ahead)
+    def _():
+        reduce_second()
 
     tree_step(feat_t, tg_send, tg_recv, 7)
+    @pl.when(behind)
+    def _():
+        reduce_first()
+
     total = jnp.zeros((ROWS, EMB), F32)
     for n in range(HID // CH):
         cols = slice(n * CH, (n + 1) * CH)
@@ -309,14 +361,6 @@
 
     over_table(lambda d, j: m_copy(d, j).start())
 
-    add((2, 0), tb, full, (in_b.at[0], 0))
-    reduce_send((2, 0), every, low, in_low, "left")
-    reduce_send((2, 0), every, high, in_high, "right")
-    add((3, 1), ta, low, (in_a1, 1))
-    reduce_send((3, 1), ta, full, in_al, "left")
-    add((1, 1), ta, high, (in_a2, 2))
-    reduce_send((1, 1), ta, full, in_ar, "right")
-
     take(z_in.at[pl.ds(0, NT - 1)], l_recv)
     take(q_in.at[pl.ds(0, NT - 1)], m_recv)
     qs_own[...] = jnp.sum(q_in[...], axis=0)
@@ -331,14 +375,41 @@
 
     lax.fori_loop(1, NC, t_start, 0)
 
-    add((3, 0), tb, full, (in_b.at[1], 3))
-    add((3, 0), every, low, (in_low, 6))
-    reduce_send((3, 0), every, full, in_l, "left")
-    add((1, 0), tb, full, (in_b.at[2], 4))
-    add((1, 0), every, high, (in_high, 7))
-    reduce_send((1, 0), every, full, in_r, "right")
-    add((0, 1), ta, full, (in_al, 8), (in_ar, 9))
-    reduce_send((0, 1), ta, full, in_ay, "y")
+    @pl.when(behind)
+    def _():
+        reduce_second()
+
+    for ref, i in ((in_b.at[3], 5), (in_l, 10), (in_r, 11), (in_ay, 12)):
+        take(ref, r_recv.at[i])
+    inv_copy.wait()
+    mine = pl.ds(pl.multiple_of(k * EB, EB), EB)
+    half = TAB // 2
+    total = gt_v[0:half, mine, :].astype(F32) + in_ay[...].astype(F32)
+    total = total + in_l[0:half].astype(F32) + in_r[0:half].astype(F32)
+    sums[0:half] = total.astype(BF16)
+    total = gt_v[half:TAB, mine, :].astype(F32) + in_b[3].astype(F32)
+    total = total + in_l[half:TAB].astype(F32) + in_r[half:TAB].astype(F32)
+    sums[half:TAB] = total.astype(BF16)
+    sums[TAB] = jnp.zeros((EB, ROWS), BF16)
+
+    def place(s, _):
+        placed[s] = sums[inv_s[s, 0]]
+        return 0
+
+    lax.fori_loop(0, SLOTS, place, 0, unroll=4)
+
+    def z_copy(d, j):
+        return remote(placed.at[pl.ds(j * LOCAL, LOCAL)], pg_in.at[:, mine, :], z_send.at[d], z_recv, c, j)
+
+    over_table(lambda d, j: z_copy(d, j).start())
+    pltpu.make_async_copy(placed.at[pl.ds(k * LOCAL, LOCAL)], pg_in.at[:, mine, :], z_recv).start()
+
+    def flip(i, _):
+        rows = pl.ds(pl.multiple_of(i * CH, CH), CH)
+        ft_out[rows, :] = jnp.transpose(feat[:, rows])
+        return 0
+
+    lax.fori_loop(0, NCHUNK, flip, 0)
 
     take(qs_in.at[pl.ds(0, NC - 1)], t_recv)
     z = jnp.sum(z_in[...], axis=0)
@@ -353,42 +424,13 @@
     for n in range(HID // EMB):
         cols = slice(n * EMB, (n + 1) * EMB)
         grad_pre = lg_col * a32_v[:, cols]
-        low_v[:, cols] = grad_pre.astype(BF16)
+        low_out[:, cols] = grad_pre.astype(BF16)
         gb_out[:, cols] = jnp.sum(grad_pre, axis=0, keepdims=True)
         gh_out[:, cols] = jnp.sum(lg_col * act_v[:, cols], axis=0, keepdims=True)
 
-    for ref, i in ((in_b.at[3], 5), (in_l, 10), (in_r, 11), (in_ay, 12)):
-        take(ref, r_recv.at[i])
-    inv_copy.wait()
-    mine = pl.ds(pl.multiple_of(k * EB, EB), EB)
-    half = TAB // 2
-    total = gt_v[0:half, mine, :].astype(F32) + in_ay[...].astype(F32)
-    total = total + in_l[0:half].astype(F32) + in_r[0:half].astype(F32)
-    sums[0:half] = (total * lg[None]).astype(BF16)
-    total = gt_v[half:TAB, mine, :].astype(F32) + in_b[3].astype(F32)
-    total = total + in_l[half:TAB].astype(F32) + in_r[half:TAB].astype(F32)
-    sums[half:TAB] = (total * lg[None]).astype(BF16)
-    sums[TAB] = jnp.zeros((EB, ROWS), BF16)
-
-    def place(s, _):
-        placed[s] = sums[inv_s[s, 0]]
-        return 0
-
-    lax.fori_loop(0, SLOTS, place, 0, unroll=4)
-
-    def z_copy(d, j):
-        return remote(placed.at[pl.ds(j * LOCAL, LOCAL)], pg_in.at[:, mine, :], z_send.at[d], z_recv, c, j)
-
-    over_table(lambda d, j: z_copy(d, j).start())
-    pltpu.make_async_copy(placed.at[pl.ds(k * LOCAL, LOCAL)], pg_in.at[:, mine, :], z_recv).start()
-
-    def gf_step(i, _):
-        rows = pl.ds(pl.multiple_of(i * CH, CH), CH)
-        g = lax.dot_general(feat[:, rows], low_v[...], (((0,), (0,)), ((), ())), preferred_element_type=F32)
-        gf_v[rows, :] = g.astype(BF16)
-        return 0
-
-    lax.fori_loop(0, NCHUNK, gf_step, 0)
+    take(pg_in, z_recv)
+    for e in range(LOCAL):
+        pg_out[e] = (pg_in[e].astype(F32) * lg).astype(BF16)
 
     over_table(lambda d, j: a_copy(d, j).wait_send())
 
@@ -401,7 +443,7 @@
 
         return 0
 
-    lax.fori_loop(0, TAB, c_wait, 0)
+    lax.fori_loop(0, NCHUNK, c_wait, 0)
     for i in range(len(TREE)):
         tree_copy(feat, ag_send, ag_recv, i).wait_send()
         tree_copy(feat_t, tg_send, tg_recv, i).wait_send()
@@ -426,19 +468,24 @@
         z_copy(d, j).wait_send()
 
     over_table(rest)
-    for copy in sends:
-        copy.wait_send()
-    take(pg_in, z_recv)
-    pg_out[...] = pg_in[...]
-
-
-def finish(gf_v, pg_v, gb_v, gh_v, loss_v, pg_out, gf_out, gb_out, gh_out, loss_out, sem):
-    copies = [pltpu.make_async_copy(gf_v, gf_out, sem.at[0]), pltpu.make_async_copy(pg_v, pg_out, sem.at[1])]
-    for copy in copies:
+    for i in range(len(messages)):
+        reduce_copy(i).wait_send()
+
+
+def finish(ft_v, low_v, pg_v, gb_v, gh_v, loss_v, pg_out, gf_out, gb_out, gh_out, loss_out, gf_v, gf_sem, pg_sem):
+    pg_copy = pltpu.make_async_copy(pg_v, pg_out, pg_sem)
+    pg_copy.start()
+    copies = []
+    for i in range(NCHUNK):
+        rows = pl.ds(i * CH, CH)
+        gf_v[rows, :] = jnp.dot(ft_v[rows, :], low_v[...], preferred_element_type=F32).astype(BF16)
+        copy = pltpu.make_async_copy(gf_v.at[rows], gf_out.at[rows], gf_sem.at[i])
         copy.start()
+        copies.append(copy)
     gb_out[...] = gb_v[...]
     gh_out[...] = gh_v[...]
     loss_out[0] = jnp.sum(loss_v[:, 0:1])
+    pg_copy.wait()
     for copy in copies:
         copy.wait()
 
@@ -452,21 +499,22 @@
     results = pl.pallas_call(
         kernel,
         out_shape=(
-            jax.ShapeDtypeStruct((FEAT, HID), BF16),
+            jax.ShapeDtypeStruct((FEAT, ROWS), BF16),
+            jax.ShapeDtypeStruct((ROWS, HID), BF16),
             jax.ShapeDtypeStruct((LOCAL, EMB, ROWS), BF16),
             jax.ShapeDtypeStruct((1, HID), F32),
             jax.ShapeDtypeStruct((1, HID), F32),
             jax.ShapeDtypeStruct((1, EMB), F32),
         ),
         in_specs=[hbm] * 7,
-        out_specs=(vmem,) * 5,
+        out_specs=(vmem,) * 6,
         scratch_shapes=[
             pltpu.VMEM((FEAT, HID), BF16),
             pltpu.VMEM((ROWS, FEAT), BF16),
             pltpu.VMEM((ROWS, FEAT), BF16),
             pltpu.VMEM((SLOTS, RB, EMB), BF16),
-            pltpu.VMEM((NC, RB, EMB), BF16),
-            pltpu.VMEM((NC, RB, EMB), BF16),
+            pltpu.VMEM((NC, RB, CH), BF16),
+            pltpu.VMEM((NC, RB, CH), BF16),
             pltpu.VMEM((ROWS, HID), F32),
             pltpu.VMEM((ROWS, HID), F32),
             pltpu.VMEM((ROWS, HID), BF16),
@@ -501,7 +549,7 @@
             dma((6,)), dma,
             dma((NT,)), dma,
             tree, tree,
-            dma((TAB,)), dma,
+            dma((NCHUNK,)), dma,
             dma((NC,)), dma,
             tree, tree,
             dma((NT,)), dma,
@@ -531,9 +579,9 @@
             jax.ShapeDtypeStruct((1, HID), F32),
             jax.ShapeDtypeStruct((1,), F32),
         ),
-        in_specs=[vmem] * 5,
+        in_specs=[vmem] * 6,
         out_specs=(hbm, hbm, vmem, vmem, smem),
-        scratch_shapes=[dma((2,))],
+        scratch_shapes=[pltpu.VMEM((FEAT, HID), BF16), dma((NCHUNK,)), dma],
         compiler_params=pltpu.CompilerParams(vmem_limit_bytes=24 * 1024 * 1024),
     )(*results)
     return pg, gf[None], gb, gh, loss

time: 79.5 us -> 77.1 us (0.970)
  Pallas kernels: 78.8 us -> 76.3 us
    pallas_call x1, Pallas kernels: 76.3 us -> 73.5 us  [on_device(): pl.pallas_call(kernel, out_shape=(jax.ShapeDtypeStruct((FEAT, ROWS), BF16...]
where the time goes in v5:
time: 77.1 us; the launch traced here: 77 us
  Pallas kernels  76.3 us (99%)
    pallas_call x1, Pallas kernels, on_device(): pl.pallas_call(kernel, out_shape=(jax.ShapeDtypeStruct((FEAT, ROWS), BF16...  73.5 us
    pallas_call x1, Pallas kernels, on_device(): pl.pallas_call(finish, out_shape=(jax.ShapeDtypeStruct((LOCAL, EMB, ROWS)...  2.79 us

profile of v5, /device:TPU:1, one launch (start us, length us, event | category | flops | bytes accessed | tf_op | source)
XLA Modules:
  0.0 77.0 jit_solution(12457367944039894489)
XLA Ops:
  0.6 73.5 %shard_map.110 = (bf16[3328,256]{1,0:T(8,128)(2,1)S(1)}, bf16[256,512]{1,0:T(8,128)(2,1)S(1)}, bf16[5,128,256]{2,1,0:T(8,128)(2,1)S(1)}, f32[1,512]{1,0:T(1,128)...) custom-call(s32[26]{0:T(128)} %slot_h.1, s32[32]{0:T(128)} %partner_h.1, s32[1,256]{1,0:T(1,128)} %bitcast.6, ...), custom_call_target="tpu_custom_call" | custom-call | tf_op jit(solution)/shard_map/pallas_call | solution.py:499
  74.2 2.8 %shard_map.111 = (bf16[5,128,256]{2,1,0:T(8,128)(2,1)}, bf16[3328,512]{1,0:T(8,128)(2,1)}, f32[1,512]{1,0:T(1,128)}, f32[1,512]{1,0:T(1,128)}, f32[1]{0:T(128)}) custom-call(bf16[3328,256]{1,0:T(8,128)(2,1)S(1)} %get-tuple-element.16.ft_v, bf16[256,512]{1,0:T(8,128)(2,1)S(1)} %get-tuple-element.17.low_v, bf16[5,128,256]{2,1,0:T(8,128)(2,1)S(1)} %get-tuple-element.18.pg_v, ...), custom_call_target="tpu_custom_call" | custom-call | tf_op jit(solution)/shard_map/pallas_call | solution.py:573

commit v6 on v5

--- a/solution.py
+++ b/solution.py
@@ -195,7 +195,7 @@
 
     all_in()
     lax.fori_loop(0, NCHUNK, c_start, 0)
-    for step in range(1, 6):
+    for step in range(1, 7):
         tree_step(feat, ag_send, ag_recv, step)
 
     my_cols = pl.ds(pl.multiple_of(my_r * CH, CH), CH)
@@ -220,8 +220,7 @@
         lax.fori_loop(1, NC, d_start, 0)
         pltpu.make_async_copy(relay_out.at[c], feat_t.at[my_rows, my_cols], d_recv).start()
 
-    for step in range(6, len(TREE_STEPS)):
-        tree_step(feat, ag_send, ag_recv, step)
+    tree_step(feat, ag_send, ag_recv, 7)
 
     def head_row(total):
         return jnp.sum(jnp.transpose(total), axis=0, keepdims=True)
@@ -321,11 +320,14 @@
     def _():
         partials()
         reduce_leaves()
-        reduce_first()
 
     take(feat_t.at[my_rows], d_recv)
     tree_step(feat_t, tg_send, tg_recv, 0)
 
+    @pl.when(ahead)
+    def _():
+        reduce_first()
+
     @pl.when(behind)
     def _():
         partials()
@@ -337,10 +339,6 @@
     @pl.when(behind)
     def _():
         reduce_leaves()
-
-    @pl.when(ahead)
-    def _():
-        reduce_second()
 
     tree_step(feat_t, tg_send, tg_recv, 7)
     @pl.when(behind)
@@ -361,6 +359,9 @@
 
     over_table(lambda d, j: m_copy(d, j).start())
 
+    reduce_second()
+
+
     take(z_in.at[pl.ds(0, NT - 1)], l_recv)
     take(q_in.at[pl.ds(0, NT - 1)], m_recv)
     qs_own[...] = jnp.sum(q_in[...], axis=0)
@@ -375,9 +376,6 @@
 
     lax.fori_loop(1, NC, t_start, 0)
 
-    @pl.when(behind)
-    def _():
-        reduce_second()
 
     for ref, i in ((in_b.at[3], 5), (in_l, 10), (in_r, 11), (in_ay, 12)):
         take(ref, r_recv.at[i])
@@ -410,6 +408,45 @@
         return 0
 
     lax.fori_loop(0, NCHUNK, flip, 0)
+
+    over_table(lambda d, j: a_copy(d, j).wait_send())
+
+    def c_wait(i, _):
+        _, to, copy = c_copy(i)
+
+        @pl.when(to != c)
+        def _():
+            copy.wait_send()
+
+        return 0
+
+    lax.fori_loop(0, NCHUNK, c_wait, 0)
+    for i in range(len(TREE)):
+        tree_copy(feat, ag_send, ag_recv, i).wait_send()
+        tree_copy(feat_t, tg_send, tg_recv, i).wait_send()
+
+    @pl.when(is_relay)
+    def _():
+        def d_wait(d, _):
+            d_copy(d, lax.rem(c + d, NC)).wait_send()
+            return 0
+
+        lax.fori_loop(1, NC, d_wait, 0)
+
+    def t_wait(d, _):
+        t_copy(d).wait_send()
+        return 0
+
+    lax.fori_loop(1, NC, t_wait, 0)
+
+    def rest(d, j):
+        l_copy(d, j).wait_send()
+        m_copy(d, j).wait_send()
+        z_copy(d, j).wait_send()
+
+    over_table(rest)
+    for i in range(len(messages)):
+        reduce_copy(i).wait_send()
 
     take(qs_in.at[pl.ds(0, NC - 1)], t_recv)
     z = jnp.sum(z_in[...], axis=0)
@@ -431,45 +468,6 @@
     take(pg_in, z_recv)
     for e in range(LOCAL):
         pg_out[e] = (pg_in[e].astype(F32) * lg).astype(BF16)
-
-    over_table(lambda d, j: a_copy(d, j).wait_send())
-
-    def c_wait(i, _):
-        _, to, copy = c_copy(i)
-
-        @pl.when(to != c)
-        def _():
-            copy.wait_send()
-
-        return 0
-
-    lax.fori_loop(0, NCHUNK, c_wait, 0)
-    for i in range(len(TREE)):
-        tree_copy(feat, ag_send, ag_recv, i).wait_send()
-        tree_copy(feat_t, tg_send, tg_recv, i).wait_send()
-
-    @pl.when(is_relay)
-    def _():
-        def d_wait(d, _):
-            d_copy(d, lax.rem(c + d, NC)).wait_send()
-            return 0
-
-        lax.fori_loop(1, NC, d_wait, 0)
-
-    def t_wait(d, _):
-        t_copy(d).wait_send()
-        return 0
-
-    lax.fori_loop(1, NC, t_wait, 0)
-
-    def rest(d, j):
-        l_copy(d, j).wait_send()
-        m_copy(d, j).wait_send()
-        z_copy(d, j).wait_send()
-
-    over_table(rest)
-    for i in range(len(messages)):
-        reduce_copy(i).wait_send()
 
 
 def finish(ft_v, low_v, pg_v, gb_v, gh_v, loss_v, pg_out, gf_out, gb_out, gh_out, loss_out, gf_v, gf_sem, pg_sem):

time: 77.1 us -> 75.8 us (0.983)
  Pallas kernels: 76.3 us -> 75 us
    pallas_call x1, Pallas kernels: 73.5 us -> 72.2 us  [on_device(): pl.pallas_call(kernel, out_shape=(jax.ShapeDtypeStruct((FEAT, ROWS), BF16...]
where the time goes in v6:
time: 75.8 us; the launch traced here: 75.7 us
  Pallas kernels  75 us (99%)
    pallas_call x1, Pallas kernels, on_device(): pl.pallas_call(kernel, out_shape=(jax.ShapeDtypeStruct((FEAT, ROWS), BF16...  72.2 us
    pallas_call x1, Pallas kernels, on_device(): pl.pallas_call(finish, out_shape=(jax.ShapeDtypeStruct((LOCAL, EMB, ROWS)...  2.79 us

profile of v6, /device:TPU:1, one launch (start us, length us, event | category | flops | bytes accessed | tf_op | source)
XLA Modules:
  0.0 75.7 jit_solution(17002636573206147653)
XLA Ops:
  0.6 72.2 %shard_map.110 = (bf16[3328,256]{1,0:T(8,128)(2,1)S(1)}, bf16[256,512]{1,0:T(8,128)(2,1)S(1)}, bf16[5,128,256]{2,1,0:T(8,128)(2,1)S(1)}, f32[1,512]{1,0:T(1,128)...) custom-call(s32[26]{0:T(128)} %slot_h.1, s32[32]{0:T(128)} %partner_h.1, s32[1,256]{1,0:T(1,128)} %bitcast.6, ...), custom_call_target="tpu_custom_call" | custom-call | tf_op jit(solution)/shard_map/pallas_call | solution.py:497
  72.9 2.8 %shard_map.111 = (bf16[5,128,256]{2,1,0:T(8,128)(2,1)}, bf16[3328,512]{1,0:T(8,128)(2,1)}, f32[1,512]{1,0:T(1,128)}, f32[1,512]{1,0:T(1,128)}, f32[1]{0:T(128)}) custom-call(bf16[3328,256]{1,0:T(8,128)(2,1)S(1)} %get-tuple-element.16.ft_v, bf16[256,512]{1,0:T(8,128)(2,1)S(1)} %get-tuple-element.17.low_v, bf16[5,128,256]{2,1,0:T(8,128)(2,1)S(1)} %get-tuple-element.18.pg_v, ...), custom_call_target="tpu_custom_call" | custom-call | tf_op jit(solution)/shard_map/pallas_call | solution.py:571

commit v7 on v6

--- a/solution.py
+++ b/solution.py
@@ -340,18 +340,23 @@
     def _():
         reduce_leaves()
 
+    def teacher(half):
+        rows = pl.ds(pl.multiple_of(half * EMB, EMB), EMB)
+        total = jnp.zeros((EMB, EMB), F32)
+        for n in range(HID // CH):
+            cols = slice(n * CH, (n + 1) * CH)
+            pre = jnp.dot(feat_t[rows, :], w_v[:, cols], preferred_element_type=F32) + b_v[:, cols].astype(F32)
+            weighed = pre * jax.nn.sigmoid(pre) * h_v[:, cols].astype(F32)
+            total = total + (weighed[:, :EMB] + weighed[:, EMB:])
+        q_own[:, rows] = head_row(total)
+
+    teacher(y)
     tree_step(feat_t, tg_send, tg_recv, 7)
     @pl.when(behind)
     def _():
         reduce_first()
 
-    total = jnp.zeros((ROWS, EMB), F32)
-    for n in range(HID // CH):
-        cols = slice(n * CH, (n + 1) * CH)
-        pre = jnp.dot(feat_t[...], w_v[:, cols], preferred_element_type=F32) + b_v[:, cols].astype(F32)
-        weighed = pre * jax.nn.sigmoid(pre) * h_v[:, cols].astype(F32)
-        total = total + (weighed[:, :EMB] + weighed[:, EMB:])
-    q_own[...] = head_row(total)
+    teacher(1 - y)
     q_in[k] = q_own[...]
 
     def m_copy(d, j):

time: 75.8 us -> 75.8 us (level)
  no operation moved by 1% of the time
where the time goes in v7:
time: 75.8 us; the launch traced here: 75.7 us
  Pallas kernels  75 us (99%)
    pallas_call x1, Pallas kernels, on_device(): pl.pallas_call(kernel, out_shape=(jax.ShapeDtypeStruct((FEAT, ROWS), BF16...  72.2 us
    pallas_call x1, Pallas kernels, on_device(): pl.pallas_call(finish, out_shape=(jax.ShapeDtypeStruct((LOCAL, EMB, ROWS)...  2.79 us

profile of v7, /device:TPU:1, one launch (start us, length us, event | category | flops | bytes accessed | tf_op | source)
XLA Modules:
  0.0 75.7 jit_solution(6958094389607461180)
XLA Ops:
  0.6 72.2 %shard_map.110 = (bf16[3328,256]{1,0:T(8,128)(2,1)S(1)}, bf16[256,512]{1,0:T(8,128)(2,1)S(1)}, bf16[5,128,256]{2,1,0:T(8,128)(2,1)S(1)}, f32[1,512]{1,0:T(1,128)...) custom-call(s32[26]{0:T(128)} %slot_h.1, s32[32]{0:T(128)} %partner_h.1, s32[1,256]{1,0:T(1,128)} %bitcast.6, ...), custom_call_target="tpu_custom_call" | custom-call | tf_op jit(solution)/shard_map/pallas_call | solution.py:502
  72.9 2.8 %shard_map.111 = (bf16[5,128,256]{2,1,0:T(8,128)(2,1)}, bf16[3328,512]{1,0:T(8,128)(2,1)}, f32[1,512]{1,0:T(1,128)}, f32[1,512]{1,0:T(1,128)}, f32[1]{0:T(128)}) custom-call(bf16[3328,256]{1,0:T(8,128)(2,1)S(1)} %get-tuple-element.16.ft_v, bf16[256,512]{1,0:T(8,128)(2,1)S(1)} %get-tuple-element.17.low_v, bf16[5,128,256]{2,1,0:T(8,128)(2,1)S(1)} %get-tuple-element.18.pg_v, ...), custom_call_target="tpu_custom_call" | custom-call | tf_op jit(solution)/shard_map/pallas_call | solution.py:576
